TPU v7x, 32 devices: a whole 2x2x4 slice. The times are simulated.
32 devices in a mesh: ctx: 2 (over x), row: 4 (over y, core), col: 4 (over z).
Axes of the slice: x: 2, y: 2, z: 4, core: 2. Of those that a mesh axis runs over, the one named last changes fastest.
Arguments:
- activations: bfloat16 [2048, 4096], P('ctx', 'col'), may hold values from -640 to 640
- norm_gain: float32 [4096], P('col'), may hold values from 0.1 to 1.9
- w_query: bfloat16 [4096, 4096], P(('row', 'ctx'), 'col'), may hold values from -0.09375 to 0.09375
- w_key: bfloat16 [4096, 4096], P(('row', 'ctx'), 'col'), may hold values from -0.09375 to 0.09375
- w_value: bfloat16 [4096, 4096], P(('row', 'ctx'), 'col'), may hold values from -0.09375 to 0.09375
- short_taps: float32 [3, 3, 4096], P(None, None, ('row', 'col')), may hold values from -2.5 to 2.5
- long_taps: float32 [128, 4096], P(None, ('row', 'col')), may hold values from -0.5 to 0.5
- skip_gain: float32 [4096], P(('row', 'col')), may hold values from -4 to 4
- w_out: bfloat16 [4096, 4096], P(('col', 'ctx'), 'row'), may hold values from -0.09375 to 0.09375
Outputs:
- mixer_out: bfloat16 [2048, 4096], P(('ctx', 'row'), 'col')
All inputs are finite; a program needn't handle non-finite values.
Results may differ from a plain program's by a relative error of at most 0.03.
Values may be sent and summed in bfloat16 or wider, within the bound.
A program may use at most 128 MiB of HBM per device.

v0:
```python
import jax
import jax.numpy as jnp
from jax import lax
from jax.sharding import PartitionSpec as P

D = 4096
SHORT_LEN = 3
FILTER_LEN = 128


epsilon = 1e-05


def tap_matrix(kernel):
    group_size = kernel.shape[0]
    width = 3 * FILTER_LEN
    padded = jnp.concatenate(
        [
            jnp.zeros((group_size, FILTER_LEN - 1), jnp.float32),
            kernel,
            jnp.zeros((group_size, FILTER_LEN + 1), jnp.float32),
        ],
        axis=1,
    )
    tiled = jnp.tile(padded, (1, FILTER_LEN + 1))
    rows = tiled[:, : FILTER_LEN * (width + 1)].reshape(group_size, FILTER_LEN, width + 1)
    return rows[:, :, : 2 * FILTER_LEN][:, :, ::-1]


def block_filter(gate_ext, tap_vals):
    channels, length = gate_ext.shape
    blocks = length // FILTER_LEN - 1
    group_size = min(channels, 32)

    def filter_group(operands):
        signal, kernel = operands
        matrix = tap_matrix(kernel)
        pieces = signal.reshape(group_size, blocks + 1, FILTER_LEN)
        joined = jnp.concatenate([pieces[:, :-1], pieces[:, 1:]], axis=2)
        result = jnp.einsum("cbi,coi->cbo", joined, matrix, precision=lax.Precision.HIGHEST)
        return result.reshape(group_size, blocks * FILTER_LEN)

    grouped = gate_ext.reshape(channels // group_size, group_size, length)
    kernels = jnp.transpose(tap_vals).reshape(channels // group_size, group_size, FILTER_LEN)
    return lax.map(filter_group, (grouped, kernels)).reshape(channels, blocks * FILTER_LEN)


def mix_channels(stacked_in, short_part, long_part_taps, skip_part):
    as_float = stacked_in.astype(jnp.float32)
    span_len = as_float.shape[2] - (SHORT_LEN - 1)
    filtered = short_part[:, 0, :, None] * as_float[:, :, SHORT_LEN - 1 : SHORT_LEN - 1 + span_len]
    for tap_idx in range(1, SHORT_LEN):
        first_pos = SHORT_LEN - 1 - tap_idx
        filtered = (
            filtered
            + short_part[:, tap_idx, :, None] * as_float[:, :, first_pos : first_pos + span_len]
        )
    query_vals = filtered[0, :, FILTER_LEN - 1 :]
    gate_vals = filtered[1] * filtered[2]
    gate_ext = jnp.concatenate([jnp.zeros((gate_vals.shape[0], 1), jnp.float32), gate_vals], axis=1)
    long_part = block_filter(gate_ext, long_part_taps)
    mixed_vals = query_vals * (long_part + skip_part[:, None] * gate_vals[:, FILTER_LEN - 1 :])
    return mixed_vals.astype(jnp.bfloat16)


def on_device(
    activations, norm_gain, w_query, w_key, w_value, short_taps, long_taps, skip_gain, w_out
):
    as_float = activations.astype(jnp.float32)
    squares = lax.psum(jnp.sum(as_float * as_float, axis=1), "col")
    normed = (as_float * lax.rsqrt(squares / D + epsilon)[:, None] * norm_gain).astype(jnp.bfloat16)
    stacked = jnp.stack([w_query, w_key, w_value])
    partial_value = jnp.einsum(
        "snd,td->snt",
        lax.all_gather(stacked, "ctx", axis=1, tiled=True),
        normed,
        preferred_element_type=jnp.float32,
    )
    qkv_vals = lax.psum_scatter(
        partial_value.astype(jnp.bfloat16), "col", scatter_dimension=1, tiled=True
    )
    prior_len = SHORT_LEN + FILTER_LEN - 2
    spread = lax.all_to_all(qkv_vals, "ctx", split_axis=1, concat_axis=2, tiled=True)
    channels = spread.shape[1]
    offset = lax.axis_index("ctx") * channels
    prior_zeros = jnp.zeros((3, channels, prior_len), jnp.bfloat16)
    mixed_chan = mix_channels(
        jnp.concatenate([prior_zeros, spread], axis=2),
        lax.dynamic_slice_in_dim(short_taps, offset, channels, 2),
        lax.dynamic_slice_in_dim(long_taps, offset, channels, 1),
        lax.dynamic_slice_in_dim(skip_gain, offset, channels, 0),
    )
    mixed_tok = lax.all_to_all(mixed_chan, "ctx", split_axis=1, concat_axis=0, tiled=True)
    block_rows = lax.all_gather(mixed_tok, "col", axis=0, tiled=True)
    out_part = lax.dot_general(
        block_rows,
        lax.all_gather(w_out, "ctx", axis=0, tiled=True),
        (((0,), (1,)), ((), ())),
        preferred_element_type=jnp.float32,
    )
    return lax.psum_scatter(out_part.astype(jnp.bfloat16), "row", scatter_dimension=0, tiled=True)


def solution(mesh):
    in_specs = (
        P("ctx", "col"),
        P("col"),
        P(("row", "ctx"), "col"),
        P(("row", "ctx"), "col"),
        P(("row", "ctx"), "col"),
        P(None, None, ("row", "col")),
        P(None, ("row", "col")),
        P(("row", "col")),
        P(("col", "ctx"), "row"),
    )
    out_specs = P(("ctx", "row"), "col")
    return jax.shard_map(
        on_device, mesh=mesh, in_specs=in_specs, out_specs=out_specs, check_vma=False
    )
```

profile of v0, /device:TPU:0, one launch (start us, length us, event | category | flops | bytes accessed | tf_op | source)
XLA Modules:
  0.0 613.2 jit_solution(3905655882688343163)
XLA Ops:
  11.2 13.5 %psum.7 = f32[1024]{0:T(1024)S(1)} all-reduce(f32[1024]{0:T(1024)S(1)} %fusion.5), channel_id=1, replica_groups=mesh['ctx'=2,'row'=4,'col'=4] {'col'}, use_global_device_ids=true, to_apply=%region_1.0 | all-reduce | flops 1024 | bytes 8192 | tf_op jit(solution)/shard_map/psum | solution.py:70
  24.6 69.2 %all-gather.4.cloned.1.call-done = bf16[3,1024,1024]{2,1,0:T(8,128)(2,1)} async-done(((bf16[3,512,1024]{2,1,0:T(8,128)(2,1)}), bf16[3,1024,1024]{2,1,0:T(8,128)(2,1)}) %all-gather.4.cloned.1.call-update) | async-done | bytes 6291472 | tf_op jit(solution)/shard_map/all_gather | solution.py:75
  93.9 11.9 %convolution_convert_fusion = bf16[3,1024,1024]{2,1,0:T(8,128)(2,1)} fusion(bf16[3,1024,1024]{2,1,0:T(8,128)(2,1)} %all-gather.4.cloned.1.call-done, bf16[1024,1024]{1,0:T(8,128)(2,1)S(1)} %copy-done.3, f32[1024]{0:T(1024)S(1)} %copy-done.4, f32[1024]{0:T(1024)S(1)} %add_rsqrt_fusion), kind=kOutput, calls=%fused_computation.14 | convolution fusion | flops 6449790976 | bytes 14688256 | tf_op jit(solution)/shard_map/snd,td->snt/dot_general | solution.py:73
  105.8 110.9 %reduce-scatter.3.cloned.1.call-done = bf16[3,256,1024]{2,1,0:T(8,128)(2,1)} async-done(((bf16[3,1024,1024]{2,1,0:T(8,128)(2,1)}), bf16[3,256,1024]{2,1,0:T(8,128)(2,1)}) %reduce-scatter.3.cloned.1.call-update) | async-done | bytes 1572880 | tf_op jit(solution)/shard_map/reduce_scatter | solution.py:79
  226.8 35.3 %all-to-all-done = bf16[3,256,1024]{2,0,1:T(4,128)(2,1)S(1)} async-done(((bf16[3,256,1024]{2,0,1:T(4,128)(2,1)}), bf16[3,256,1024]{2,0,1:T(4,128)(2,1)S(1)}, u32[]{:S(2)}, u32[]{:S(2)}) %all-to-all-start) | async-done | bytes 1572896 | tf_op jit(solution)/shard_map/all_to_all | solution.py:83
  271.9 239.3 %while.10 = (s32[]{:T(128)}, f32[4,32,2048]{2,1,0:T(8,128)}, f32[4,32,2176]{2,1,0:T(8,128)S(1)}, f32[4,32,128]{2,1,0:T(8,128)S(1)}, s32[]{:T(128)}, /*index=5*/f32[]{:T(128)}, f32[]{:T(128)}) while((s32[]{:T(128)}, f32[4,32,2048]{2,1,0:T(8,128)}, f32[4,32,2176]{2,1,0:T(8,128)S(1)}, f32[4,32,128]{2,1,0:T(8,128)S(1)}, s32[]{:T(128)}, ...), condition=%wide.region_4.5_spmd, body=%wide.region_3.4_spmd.sunk | while | flops 201482240 | bytes 69378160 | solution.py:45
  276.8 9.9 %reshape.38 = f32[32,128,385]{2,1,0:T(8,128)} reshape(f32[32,49280]{1,0:T(8,128)} %slice.96) | data formatting | bytes 12615680 | tf_op jit(solution)/shard_map/while/body/eval_jaxpr/reshape | solution.py:26
  286.7 4.6 slice.97
  291.3 34.2 %rev.4 = f32[32,128,256]{2,1,0:T(8,128)} reverse(f32[32,128,256]{2,1,0:T(8,128)} %slice.97), dimensions={2} | reverse | bytes 8388608 | tf_op jit(solution)/shard_map/while/body/eval_jaxpr/rev | solution.py:27
  325.7 5.3 fusion.30
  336.6 9.9 %reshape.38 = f32[32,128,385]{2,1,0:T(8,128)} reshape(f32[32,49280]{1,0:T(8,128)} %slice.96) | data formatting | bytes 12615680 | tf_op jit(solution)/shard_map/while/body/eval_jaxpr/reshape | solution.py:26
  346.5 4.6 slice.97
  351.1 34.2 %rev.4 = f32[32,128,256]{2,1,0:T(8,128)} reverse(f32[32,128,256]{2,1,0:T(8,128)} %slice.97), dimensions={2} | reverse | bytes 8388608 | tf_op jit(solution)/shard_map/while/body/eval_jaxpr/rev | solution.py:27
  385.5 5.3 fusion.30
  396.4 9.9 %reshape.38 = f32[32,128,385]{2,1,0:T(8,128)} reshape(f32[32,49280]{1,0:T(8,128)} %slice.96) | data formatting | bytes 12615680 | tf_op jit(solution)/shard_map/while/body/eval_jaxpr/reshape | solution.py:26
  411.0 34.2 %rev.4 = f32[32,128,256]{2,1,0:T(8,128)} reverse(f32[32,128,256]{2,1,0:T(8,128)} %slice.97), dimensions={2} | reverse | bytes 8388608 | tf_op jit(solution)/shard_map/while/body/eval_jaxpr/rev | solution.py:27
  445.3 5.3 fusion.30
  456.2 9.9 %reshape.38 = f32[32,128,385]{2,1,0:T(8,128)} reshape(f32[32,49280]{1,0:T(8,128)} %slice.96) | data formatting | bytes 12615680 | tf_op jit(solution)/shard_map/while/body/eval_jaxpr/reshape | solution.py:26
  470.8 34.2 %rev.4 = f32[32,128,256]{2,1,0:T(8,128)} reverse(f32[32,128,256]{2,1,0:T(8,128)} %slice.97), dimensions={2} | reverse | bytes 8388608 | tf_op jit(solution)/shard_map/while/body/eval_jaxpr/rev | solution.py:27
  505.1 5.3 fusion.30
  514.4 9.7 %all_to_all.37 = bf16[128,2,1024]{2,0,1:T(8,128)(2,1)} all-to-all(bf16[128,2,1024]{2,0,1:T(8,128)(2,1)S(1)} %copy.32), channel_id=1, replica_groups=mesh['ctx'=2,'row'=4,'col'=4] {'ctx'}, dimensions={1} | all-to-all | bytes 1048576 | tf_op jit(solution)/shard_map/all_to_all | solution.py:93
  524.5 45.9 %all-gather.6.cloned.1.call-done = bf16[1024,1024]{1,0:T(8,128)(2,1)} async-done(((bf16[256,1024]{1,0:T(8,128)(2,1)}), bf16[1024,1024]{1,0:T(8,128)(2,1)}) %all-gather.6.cloned.1.call-update) | async-done | bytes 2097168 | tf_op jit(solution)/shard_map/all_gather | solution.py:94
  570.4 6.0 convolution_convert_fusion.1
  576.4 30.3 %reduce-scatter.5.cloned.1.call-done = bf16[256,1024]{1,0:T(8,128)(2,1)} async-done(((bf16[1024,1024]{1,0:T(8,128)(2,1)}), bf16[256,1024]{1,0:T(8,128)(2,1)}) %reduce-scatter.5.cloned.1.call-update) | async-done | bytes 524304 | tf_op jit(solution)/shard_map/reduce_scatter | solution.py:101
  (103 shorter events, 60.0 us)
Async XLA Ops:
  6.5 220.0 %copy-start = (f32[128,256]{1,0:T(8,128)S(1)}, f32[128,256]{1,0:T(8,128)}, u32[]{:S(2)}) copy-start(f32[128,256]{1,0:T(8,128)} %param.17) | copy-start | bytes 393220
  6.5 87.3 %all-gather.4.cloned.1.call-start = ((), (), s32[]{:S(2)}) async-start(), calls=%async_computation.4 | async-start | bytes 9437184 | tf_op jit(solution)/shard_map/all_gather | solution.py:75
  6.5 4.1 copy-start.3
  10.6 83.3 %copy-start.4 = (f32[1024]{0:T(1024)S(1)}, f32[1024]{0:T(1024)}, u32[]{:S(2)}) copy-start(f32[1024]{0:T(1024)} %param.12) | copy-start | bytes 12292
  10.6 206.1 %reduce-scatter.3.cloned.1.call-start = ((), (), s32[]{:S(2)}) async-start(), calls=%async_computation.5 | async-start | bytes 7864320 | tf_op jit(solution)/shard_map/reduce_scatter | solution.py:79
  220.8 5.9 copy-start.5
  220.8 41.3 %all-to-all-start = ((bf16[3,256,1024]{2,0,1:T(4,128)(2,1)}), bf16[3,256,1024]{2,0,1:T(4,128)(2,1)S(1)}, u32[]{:S(2)}, u32[]{:S(2)}) async-start(bf16[3,256,1024]{2,0,1:T(4,128)(2,1)} %copy.26), calls=%async_computation.1 | async-start | bytes 4194304 | tf_op jit(solution)/shard_map/all_to_all | solution.py:83
  224.7 299.8 %all-gather.8.cloned.1.call-start = ((), (), s32[]{:S(2)}) async-start(), calls=%async_computation.7 | async-start | bytes 3145728 | tf_op jit(solution)/shard_map/all_gather | solution.py:97
  225.4 345.0 %all-gather.6.cloned.1.call-start = ((), (), s32[]{:S(2)}) async-start(), calls=%async_computation.6 | async-start | bytes 2621440 | tf_op jit(solution)/shard_map/all_gather | solution.py:94
  267.1 1.7 copy-start.2
  524.2 82.5 %reduce-scatter.5.cloned.1.call-start = ((), (), s32[]{:S(2)}) async-start(), calls=%async_computation.8 | async-start | bytes 2621440 | tf_op jit(solution)/shard_map/reduce_scatter | solution.py:101
  570.4 36.3 %copy-start.1 = (f32[128,256]{1,0:T(8,128)S(1)}, f32[128,256]{1,0:T(8,128)}, u32[]{:S(2)}) copy-start(f32[128,256]{1,0:T(8,128)} %param.17) | copy-start | bytes 393220
Sparse Core Ops, SparseCore 0:
  10.7 83.0 all-gather.3
  105.9 110.7 reduce-scatter.2
  227.1 45.4 all-gather.7
  524.3 46.0 all-gather.5
  576.5 30.1 reduce-scatter.4
where the time goes:
time: 624 us; the launch traced here: 613 us
  waiting for transfers between devices  292 us (47%)
  local copies, waits for them, and re-layouts  233 us (37%)
  matrix products  39 us (6%)
  blocking collectives  23.2 us (4%)
  between operations  13.3 us (2%)
  other arithmetic  7.77 us (1%)
    rev x4, local copies, waits for them, and re-layouts, tap_matrix(): return rows[:, :, :2 * FILTER_LEN][:, :, ::-1]  137 us
    reduce_scatter x1, waiting for transfers between devices, on_device(): lax.psum_scatter(partial_value.astype(jnp.bfloat16), 'col', scatter_dimen...  111 us
    all_gather x1, waiting for transfers between devices, on_device(): lax.all_gather(stacked, 'ctx', axis=1, tiled=True)  69.2 us
    all_gather x1, waiting for transfers between devices, on_device(): block_rows = lax.all_gather(mixed_tok, 'col', axis=0, tiled=True)  45.9 us
    reshape x4, local copies, waits for them, and re-layouts, tap_matrix(): tiled[:, :FILTER_LEN * (width + 1)]  39.8 us
    all_to_all x1, waiting for transfers between devices, on_device(): lax.all_to_all(qkv_vals, 'ctx', split_axis=1, concat_axis=2, tiled=True)  35.3 us
    reduce_scatter x1, waiting for transfers between devices, on_device(): lax.psum_scatter(out_part.astype(jnp.bfloat16), 'row', scatter_dimension=...  30.3 us
    dot_general x4, matrix products, filter_group(): jnp.einsum('cbi,coi->cbo', joined, matrix, precision=lax.Precision.HIGHEST)  21.2 us
  transfers between devices with their start and end apart: 6, of which 5 were waited for; matrix products, arithmetic and copies ran while one was open for 41% of the time, Pallas kernels for 0%

commit v1 on v0

v1 whole, which is shorter than its diff:
```python
import functools

import jax
import jax.numpy as jnp
from jax import lax
from jax.experimental import pallas as pl
from jax.experimental.pallas import tpu as pltpu
from jax.sharding import PartitionSpec as P

D = 4096
SHORT_LEN = 3
FILTER_LEN = 128
SUB = 8
epsilon = 1e-05


def filter_kernel(x_ref, scale_ref, short_ref, long_ref, skip_ref, out_ref, prev, gates, shifted):
    step = pl.program_id(0)
    rows = x_ref.shape[1]

    @pl.when(step == 0)
    def _():
        prev[...] = jnp.zeros_like(prev)
        gates[0:SUB, :] = jnp.zeros((SUB, gates.shape[1]), jnp.float32)
        shifted[:, 0:FILTER_LEN, :] = jnp.zeros((SUB, FILTER_LEN, shifted.shape[2]), jnp.float32)

    @pl.when(step > 0)
    def _():
        shifted[:, 0:FILTER_LEN, :] = shifted[:, rows : rows + FILTER_LEN, :]

    filtered = []
    for which in range(3):
        now = x_ref[which].astype(jnp.float32) * scale_ref[...]
        prev[which, SUB:, :] = now
        total = short_ref[which, 0:1, :] * now
        for tap in range(1, SHORT_LEN):
            total = total + short_ref[which, tap : tap + 1, :] * prev[which, SUB - tap : SUB - tap + rows, :]
        filtered.append(total)
        prev[which, 0:SUB, :] = prev[which, rows : rows + SUB, :]
    gate = filtered[1] * filtered[2]
    gates[SUB:, :] = gate
    for move in range(SUB):
        shifted[move, FILTER_LEN:, :] = gates[SUB - move : SUB - move + rows, :]
    gates[0:SUB, :] = gates[rows : rows + SUB, :]
    total = skip_ref[...] * gate
    for move in range(SUB):
        for back in range(0, FILTER_LEN, SUB):
            total = total + long_ref[back + move : back + move + 1, :] * shifted[
                move, FILTER_LEN - back : FILTER_LEN - back + rows, :
            ]
    out_ref[...] = (filtered[0] * total).astype(out_ref.dtype)


def mix(stacked, scale, short_taps, long_taps, skip_gain):
    _, tokens, channels = stacked.shape
    rows = FILTER_LEN
    return pl.pallas_call(
        filter_kernel,
        grid=(tokens // rows,),
        in_specs=[
            pl.BlockSpec((3, rows, channels), lambda i: (0, i, 0)),
            pl.BlockSpec((rows, 1), lambda i: (i, 0)),
            pl.BlockSpec((3, SHORT_LEN, channels), lambda i: (0, 0, 0)),
            pl.BlockSpec((FILTER_LEN, channels), lambda i: (0, 0)),
            pl.BlockSpec((1, channels), lambda i: (0, 0)),
        ],
        out_specs=pl.BlockSpec((rows, channels), lambda i: (i, 0)),
        out_shape=jax.ShapeDtypeStruct((tokens, channels), jnp.bfloat16),
        scratch_shapes=[
            pltpu.VMEM((3, SUB + rows, channels), jnp.float32),
            pltpu.VMEM((SUB + rows, channels), jnp.float32),
            pltpu.VMEM((SUB, FILTER_LEN + rows, channels), jnp.float32),
        ],
    )(stacked, scale, short_taps, long_taps, skip_gain)


def shift(value, axis, size, by):
    return lax.ppermute(value, axis, [((i + by) % size, i) for i in range(size)])


def on_device(
    n_ctx, n_row, n_col,
    activations, norm_gain, w_query, w_key, w_value, short_taps, long_taps, skip_gain, w_out,
):
    ctx, col = lax.axis_index("ctx"), lax.axis_index("col")
    tokens, features = activations.shape
    held = w_query.shape[0]
    width = held // n_col
    stacked = jnp.stack([w_query, w_key, w_value]).reshape(3, n_col, width, features)

    taps = jnp.concatenate([short_taps.reshape(9, -1), long_taps, skip_gain[None]], axis=0)
    taps = lax.all_gather(taps, "col", axis=1, tiled=True)
    taps = lax.dynamic_slice_in_dim(taps, ctx * held + col * width, width, 1)

    w_full = lax.all_gather(w_out, "ctx", axis=0, tiled=True)
    w_full = jnp.transpose(w_full.reshape(-1, n_ctx, n_col, width), (0, 2, 1, 3)).reshape(w_full.shape)

    qkv = jnp.zeros((3, n_ctx * tokens, width), jnp.bfloat16)
    squares = jnp.zeros((n_ctx * tokens,), jnp.float32)
    for step in range(n_ctx):
        part = activations if step == 0 else shift(activations, "ctx", n_ctx, step)
        first = lax.rem(ctx + step, n_ctx) * tokens
        as_float = part.astype(jnp.float32)
        squares = lax.dynamic_update_slice(squares, jnp.sum(as_float * as_float, axis=1), (first,))
        scaled = (as_float * norm_gain).astype(jnp.bfloat16)
        partial_value = jnp.einsum("td,skcd->kstc", scaled, stacked, preferred_element_type=jnp.float32)
        summed = lax.psum_scatter(partial_value.astype(jnp.bfloat16), "col", scatter_dimension=0, tiled=True)
        qkv = lax.dynamic_update_slice(qkv, summed[0], (0, first, 0))

    total = squares.reshape(-1, 128)
    for step in range(1, n_col):
        total = total + shift(squares.reshape(-1, 128), "col", n_col, step)
    scale = lax.rsqrt(total / D + epsilon).reshape(-1, 1)

    mixed = mix(qkv, scale, taps[:9].reshape(3, 3, width), taps[9:-1], taps[-1:])

    spread = lax.all_to_all(
        mixed.reshape(n_ctx, tokens, width), "ctx", split_axis=0, concat_axis=0, tiled=True
    )
    spread = jnp.transpose(spread, (1, 0, 2)).reshape(tokens, n_ctx * width)
    block_rows = lax.all_gather(spread, "col", axis=1, tiled=True)
    out_part = lax.dot_general(
        block_rows, w_full, (((1,), (1,)), ((), ())), preferred_element_type=jnp.float32
    )
    return lax.psum_scatter(out_part.astype(jnp.bfloat16), "row", scatter_dimension=0, tiled=True)


def solution(mesh):
    in_specs = (
        P("ctx", "col"),
        P("col"),
        P(("row", "ctx"), "col"),
        P(("row", "ctx"), "col"),
        P(("row", "ctx"), "col"),
        P(None, None, ("row", "col")),
        P(None, ("row", "col")),
        P(("row", "col")),
        P(("col", "ctx"), "row"),
    )
    out_specs = P(("ctx", "row"), "col")
    body = functools.partial(on_device, mesh.shape["ctx"], mesh.shape["row"], mesh.shape["col"])
    return jax.shard_map(body, mesh=mesh, in_specs=in_specs, out_specs=out_specs, check_vma=False)
```

time: 624 us -> 264 us (0.42); the launches traced: 613 us -> 264 us
  local copies, waits for them, and re-layouts: 233 us -> 16.4 us
  waiting for transfers between devices: 292 us -> 157 us
  matrix products: 39 us -> 18.8 us
  Pallas kernels: 0 us -> 16.6 us
  blocking collectives: 23.2 us -> 32 us
  other arithmetic: 7.77 us -> 0.98 us
    rev x4 -> x0, local copies, waits for them, and re-layouts: 137 us -> none  [tap_matrix(): return rows[:, :, :2 * FILTER_LEN][:, :, ::-1]]
    reduce_scatter x1 -> x2, waiting for transfers between devices: 111 us -> 35.2 us  [on_device(): lax.psum_scatter(partial_value.astype(jnp.bfloat16), 'col', scatter_dimen...]
    all_gather x3 -> x2, waiting for transfers between devices: 115 us -> 43.3 us  [the longest x1 43.3 us: on_device(): block_rows = lax.all_gather(spread, 'col', axis=1, tiled=True)]
    ppermute x0 -> x4, waiting for transfers between devices: none -> 48.6 us  [shift(): lax.ppermute(value, axis, [((i + by) % size, i) for i in range(size)])]
    reshape x9 -> x4, local copies, waits for them, and re-layouts: 41.5 us -> 3.3 us  [the longest x1 1.45 us: on_device(): scale = lax.rsqrt(total / D + epsilon).reshape(-1, 1)]
    all_to_all x1 -> x0, waiting for transfers between devices: 35.3 us -> none  [on_device(): lax.all_to_all(qkv_vals, 'ctx', split_axis=1, concat_axis=2, tiled=True)]
    slice x13 -> x3, local copies, waits for them, and re-layouts: 31.9 us -> 1.38 us  [the longest x1 0.72 us: on_device(): taps[9:-1]]
    all_gather x0 -> x1, blocking collectives: none -> 20.4 us  [on_device(): taps = lax.all_gather(taps, 'col', axis=1, tiled=True)]
  transfers between devices with their start and end apart: 6 -> 9, of which waited for: 5 -> 6; matrix products, arithmetic and copies ran while one was open for 41% -> 7% of each run, Pallas kernels for 0% -> 6%
where the time goes in v1:
time: 264 us
  waiting for transfers between devices  157 us (59%)
  blocking collectives  32 us (12%)
  matrix products  18.8 us (7%)
  Pallas kernels  16.6 us (6%)
  local copies, waits for them, and re-layouts  16.4 us (6%)
  between operations  15.2 us (6%)
  starting transfers between devices  6.28 us (2%)
    ppermute x4, waiting for transfers between devices, shift(): lax.ppermute(value, axis, [((i + by) % size, i) for i in range(size)])  48.6 us
    all_gather x1, waiting for transfers between devices, on_device(): block_rows = lax.all_gather(spread, 'col', axis=1, tiled=True)  43.3 us
    reduce_scatter x2, waiting for transfers between devices, on_device(): lax.psum_scatter(partial_value.astype(jnp.bfloat16), 'col', scatter_dimen...  35.2 us
    reduce_scatter x1, waiting for transfers between devices, on_device(): lax.psum_scatter(out_part.astype(jnp.bfloat16), 'row', scatter_dimension=...  30.3 us
    all_gather x1, blocking collectives, on_device(): taps = lax.all_gather(taps, 'col', axis=1, tiled=True)  20.4 us
    pallas_call x1, Pallas kernels, mix(): pl.pallas_call(filter_kernel, grid=(tokens // rows,), in_specs=[pl.BlockS...  16.6 us
    dot_general x2, matrix products, on_device(): jnp.einsum('td,skcd->kstc', scaled, stacked, preferred_element_type=jnp.f...  13.5 us
    all_to_all x1, blocking collectives, on_device(): lax.all_to_all(mixed.reshape(n_ctx, tokens, width), 'ctx', split_axis=0,...  11.7 us
  transfers between devices with their start and end apart: 9, of which 6 were waited for; matrix products, arithmetic and copies ran while one was open for 7% of the time, Pallas kernels for 6%

profile of v1, /device:TPU:0, one launch (start us, length us, event | category | flops | bytes accessed | tf_op | source)
XLA Modules:
  0.0 263.6 jit_solution(18255215951837056974)
XLA Ops:
  7.4 7.1 %convert_bitcast_fusion.1 = bf16[4,3,1024,128]{3,2,1,0:T(8,128)(2,1)} fusion(bf16[1024,1024]{1,0:T(8,128)(2,1)} %param.9, f32[1024]{0:T(1024)} %param.10, bf16[1,4,128,1024]{3,2,1,0:T(8,128)(2,1)} %bitcast.40, bf16[1,4,128,1024]{3,2,1,0:T(8,128)(2,1)} %bitcast.42, bf16[1,4,128,1024]{3,2,1,0:T(8,128)(2,1)} %bitcast.44), kind=kOutput, calls=%fused_computation.10 | convolution fusion | flops 3229089792 | bytes 8392704 | tf_op jit(solution)/shard_map/td,skcd->kstc/dot_general | solution.py:106
  14.6 1.5 copy-done.1
  16.1 2.9 %collective-permute-start = (bf16[1024,1024]{1,0:T(8,128)(2,1)S(1)}, bf16[1024,1024]{1,0:T(8,128)(2,1)S(1)}, u32[]{:S(2)}, u32[]{:S(2)}) collective-permute-start(bf16[1024,1024]{1,0:T(8,128)(2,1)S(1)} %copy-done.1), channel_id=1, source_target_pairs={{16,0},{0,16},{17,1},{1,17},{18,2},{2,18},{19,3},{3,19},{20,4},{4,... | collective-permute-start | bytes 6291464 | tf_op jit(solution)/shard_map/ppermute | solution.py:78
  19.0 45.6 %collective-permute-done = bf16[1024,1024]{1,0:T(8,128)(2,1)S(1)} collective-permute-done((bf16[1024,1024]{1,0:T(8,128)(2,1)S(1)}, bf16[1024,1024]{1,0:T(8,128)(2,1)S(1)}, u32[]{:S(2)}, u32[]{:S(2)}) %collective-permute-start) | collective-permute-done | bytes 2097184 | tf_op jit(solution)/shard_map/ppermute | solution.py:78
  64.6 1.4 copy-done.2
  66.0 6.4 %convert_bitcast_fusion = bf16[4,3,1024,128]{3,2,1,0:T(8,128)(2,1)} fusion(bf16[1024,1024]{1,0:T(8,128)(2,1)S(1)} %collective-permute-done, f32[1024]{0:T(1024)S(1)} %copy-done.9, bf16[1,4,128,1024]{3,2,1,0:T(8,128)(2,1)S(1)} %bitcast.41, bf16[1,4,128,1024]{3,2,1,0:T(8,128)(2,1)} %bitcast.43, bf16[1,4,128,1024]{3,2,1,0:T(8,128)(2,1)} %bitcast.45), kind=kOutput, calls=%fused_computation.9 | convolution fusion | flops 3229089792 | bytes 8392704 | tf_op jit(solution)/shard_map/td,skcd->kstc/dot_general | solution.py:106
  72.5 1.1 copy-done.4
  73.7 1.3 copy.20
  75.9 20.4 %all_gather.9 = f32[138,1024]{1,0:T(8,128)S(1)} all-gather(f32[138,256]{1,0:T(8,128)S(1)} %pad_maximum_fusion.1), channel_id=1, replica_groups=mesh['ctx'=2,'row'=4,'col'=4] {'col'}, dimensions={1}, use_global_device_ids=true | all-gather | bytes 706560 | tf_op jit(solution)/shard_map/all_gather | solution.py:92
  97.1 2.5 collective-permute-start.1
  102.2 2.1 collective-permute-done.2
  104.3 0.9 collective-permute-done.3
  105.2 1.4 copy.18.scale_ref
  106.9 1.2 bitcast_dynamic-update-slice_fusion.1
  108.1 35.2 %reduce-scatter.6.cloned.1.call-done = bf16[1,3,1024,128]{3,2,1,0:T(8,128)(2,1)} async-done(((bf16[4,3,1024,128]{3,2,1,0:T(8,128)(2,1)}), bf16[1,3,1024,128]{3,2,1,0:T(8,128)(2,1)}) %reduce-scatter.6.cloned.1.call-update) | async-done | bytes 786448 | tf_op jit(solution)/shard_map/reduce_scatter | solution.py:107
  143.3 1.2 bitcast_dynamic-update-slice_fusion.x_ref
  144.5 1.2 copy-done
  145.7 16.6 %shard_map.91 = bf16[2048,128]{1,0:T(8,128)(2,1)} custom-call(bf16[3,2048,128]{2,1,0:T(8,128)(2,1)} %copy-done, f32[2048,1]{1,0:T(8,128)} %copy.18.scale_ref, f32[3,3,128]{2,1,0:T(4,128)} %reshape.38.short_ref, f32[128,128]{1,0:T(8,128)} %dynamic-slice.1.long_ref, f32[1,128]{1,0:T(1,128)} %dynamic-slice.2.skip_ref), custom_call_target="tpu_custom_call" | custom-call | tf_op jit(solution)/shard_map/pallas_call | solution.py:57
  162.3 1.2 copy.19
  163.5 11.7 %all_to_all.5 = bf16[2,1024,128]{1,2,0:T(8,128)(2,1)} all-to-all(bf16[2,1024,128]{1,2,0:T(8,128)(2,1)S(1)} %copy.19), channel_id=1, replica_groups=mesh['ctx'=2,'row'=4,'col'=4] {'ctx'}, dimensions={0} | all-to-all | bytes 1048576 | tf_op jit(solution)/shard_map/all_to_all | solution.py:117
  175.3 1.9 copy.21
  177.2 43.3 %all-gather.3.cloned.1.call-done = bf16[1024,1024]{0,1:T(8,128)(2,1)} async-done(((bf16[1024,256]{0,1:T(8,128)(2,1)}), bf16[1024,1024]{0,1:T(8,128)(2,1)}) %all-gather.3.cloned.1.call-update) | async-done | bytes 2097168 | tf_op jit(solution)/shard_map/all_gather | solution.py:121
  220.5 5.3 %convolution_convert_fusion = bf16[1024,1024]{1,0:T(8,128)(2,1)} fusion(bf16[1024,1024]{0,1:T(8,128)(2,1)} %all-gather.3.cloned.1.call-done, bf16[1024,1024]{0,1:T(8,128)(2,1)S(1)} %bitcast.32), kind=kOutput, calls=%fused_computation.19 | convolution fusion | flops 2148532224 | bytes 6291456 | tf_op jit(solution)/shard_map/dot_general | solution.py:122
  225.8 30.3 %reduce-scatter.8.cloned.1.call-done = bf16[256,1024]{1,0:T(8,128)(2,1)} async-done(((bf16[1024,1024]{1,0:T(8,128)(2,1)}), bf16[256,1024]{1,0:T(8,128)(2,1)}) %reduce-scatter.8.cloned.1.call-update) | async-done | bytes 524304 | tf_op jit(solution)/shard_map/reduce_scatter | solution.py:125
  (44 shorter events, 4.7 us)
Async XLA Ops:
  7.4 99.3 %reduce-scatter.4.cloned.1.call-start = ((), (), s32[]{:S(2)}) async-start(), calls=%async_computation.4 | async-start | bytes 3932160 | tf_op jit(solution)/shard_map/reduce_scatter | solution.py:107
  7.4 58.6 %copy-start.9 = (f32[1024]{0:T(1024)S(1)}, f32[1024]{0:T(1024)}, u32[]{:S(2)}) copy-start(f32[1024]{0:T(1024)} %param.10) | copy-start | bytes 12292
  14.5 1.6 copy-start.1
  14.5 51.5 %copy-start.8 = (bf16[512,1024]{1,0:T(8,128)(2,1)S(1)}, bf16[512,1024]{1,0:T(8,128)(2,1)}, u32[]{:S(2)}) copy-start(bf16[512,1024]{1,0:T(8,128)(2,1)} %param.13) | copy-start | bytes 3145732
  14.5 128.8 %reduce-scatter.6.cloned.1.call-start = ((), (), s32[]{:S(2)}) async-start(), calls=%async_computation.5 | async-start | bytes 3932160 | tf_op jit(solution)/shard_map/reduce_scatter | solution.py:107
  16.1 48.6 %collective-permute-start = (bf16[1024,1024]{1,0:T(8,128)(2,1)S(1)}, bf16[1024,1024]{1,0:T(8,128)(2,1)S(1)}, u32[]{:S(2)}, u32[]{:S(2)}) collective-permute-start(bf16[1024,1024]{1,0:T(8,128)(2,1)S(1)} %copy-done.1), channel_id=1, source_target_pairs={{16,0},{0,16},{17,1},{1,17},{18,2},{2,18},{19,3},{3,19},{20,4},{4,... | collective-permute-start | bytes 6291464 | tf_op jit(solution)/shard_map/ppermute | solution.py:78
  64.6 1.4 copy-start.2
  72.4 1.3 copy-start.4
  72.4 2.7 %copy-start.6 = (f32[3,3,256]{2,1,0:T(4,128)S(1)}, f32[3,3,256]{2,1,0:T(4,128)}, u32[]{:S(2)}) copy-start(f32[3,3,256]{2,1,0:T(4,128)} %param.14) | copy-start | bytes 27652
  72.4 3.5 %copy-start.5 = (f32[128,256]{1,0:T(8,128)S(1)}, f32[128,256]{1,0:T(8,128)}, u32[]{:S(2)}) copy-start(f32[128,256]{1,0:T(8,128)} %param.15) | copy-start | bytes 393220
  72.5 3.5 %copy-start.7 = (f32[256]{0:T(256)S(1)}, f32[256]{0:T(256)}, u32[]{:S(2)}) copy-start(f32[256]{0:T(256)} %param.16) | copy-start | bytes 3076
  72.5 102.8 %all-gather.5.cloned.1.call-start = ((), (), s32[]{:S(2)}) async-start(), calls=%async_computation.7 | async-start | bytes 3145728 | tf_op jit(solution)/shard_map/all_gather | solution.py:95
  75.0 145.4 %all-gather.3.cloned.1.call-start = ((), (), s32[]{:S(2)}) async-start(), calls=%async_computation.6 | async-start | bytes 2621440 | tf_op jit(solution)/shard_map/all_gather | solution.py:121
  75.1 21.2 %copy-start.3 = (bf16[1024,1024]{1,0:T(8,128)(2,1)S(1)}, bf16[1024,1024]{1,0:T(8,128)(2,1)}, u32[]{:S(2)}) copy-start(bf16[1024,1024]{1,0:T(8,128)(2,1)} %copy-done.2) | copy-start | bytes 6291460
  97.1 5.2 %collective-permute-start.1 = (f32[16,128]{1,0:T(8,128)S(1)}, f32[16,128]{1,0:T(8,128)S(1)}, u32[]{:S(2)}, u32[]{:S(2)}) collective-permute-start(f32[16,128]{1,0:T(8,128)S(1)} %bitcast.36), channel_id=1, source_target_pairs={{1,0},{2,1},{3,2},{0,3},{5,4},{6,5},{7,6},{4,7},{9,8},{10,9},{11,1... | collective-permute-start | bytes 24584 | tf_op jit(solution)/shard_map/ppermute | solution.py:78
  99.6 4.7 %collective-permute-start.2 = (f32[16,128]{1,0:T(8,128)S(1)}, f32[16,128]{1,0:T(8,128)S(1)}, u32[]{:S(2)}, u32[]{:S(2)}) collective-permute-start(f32[16,128]{1,0:T(8,128)S(1)} %bitcast.37), channel_id=1, source_target_pairs={{2,0},{3,1},{0,2},{1,3},{6,4},{7,5},{4,6},{5,7},{10,8},{11,9},{8,1... | collective-permute-start | bytes 24584 | tf_op jit(solution)/shard_map/ppermute | solution.py:78
  99.6 5.6 %collective-permute-start.3 = (f32[16,128]{1,0:T(8,128)S(1)}, f32[16,128]{1,0:T(8,128)S(1)}, u32[]{:S(2)}, u32[]{:S(2)}) collective-permute-start(f32[16,128]{1,0:T(8,128)S(1)} %bitcast.38), channel_id=1, source_target_pairs={{3,0},{0,1},{1,2},{2,3},{7,4},{4,5},{5,6},{6,7},{11,8},{8,9},{9,10... | collective-permute-start | bytes 24584 | tf_op jit(solution)/shard_map/ppermute | solution.py:78
  144.5 1.2 copy-start
  175.2 80.8 %reduce-scatter.8.cloned.1.call-start = ((), (), s32[]{:S(2)}) async-start(), calls=%async_computation.8 | async-start | bytes 2621440 | tf_op jit(solution)/shard_map/reduce_scatter | solution.py:125
Sparse Core Ops, SparseCore 0:
  14.6 62.9 reduce-scatter.3
  79.9 63.3 reduce-scatter.5
Sparse Core Ops, SparseCore 1:
  75.1 34.5 all-gather.4
  175.3 45.1 all-gather.2
  225.9 30.1 reduce-scatter.7

commit v2 on v1

--- a/solution.py
+++ b/solution.py
@@ -125,6 +125,293 @@
     return lax.psum_scatter(out_part.astype(jnp.bfloat16), "row", scatter_dimension=0, tiled=True)
 
 
+def chain_kernel(
+    last, x_ref, gain_ref, w_ref, scale_ref, taps_ref, out_ref,
+    xs, acc, prev, gates, shifted, stage, gath,
+    acc_send, acc_recv, x_send, x_recv, stage_send, stage_recv, z_send, z_recv,
+):
+    ctx, col = lax.axis_index("ctx"), lax.axis_index("col")
+    pieces = xs.shape[1]
+    chunks = acc.shape[1]
+    rows = xs.shape[2]
+    width = gath.shape[4]
+    is_end = (col == 0) | (col == last)
+    end_half = jnp.where(col == 0, 0, 1)
+    inward = jnp.where(col == 0, 1, last - 1)
+    left, right = jnp.maximum(col - 1, 0), jnp.minimum(col + 1, last)
+    peer = {"ctx": 1 - ctx}
+    mesh_ids = pl.DeviceIdType.MESH
+
+    xs[0] = (x_ref[...].astype(jnp.float32) * gain_ref[...]).astype(jnp.bfloat16).reshape(xs.shape[1:])
+
+    barrier = pltpu.get_barrier_semaphore()
+    pl.semaphore_signal(barrier, inc=1, device_id=peer, device_id_type=mesh_ids)
+
+    @pl.when(col > 0)
+    def _():
+        pl.semaphore_signal(barrier, inc=1, device_id={"col": left}, device_id_type=mesh_ids)
+
+    @pl.when(col < last)
+    def _():
+        pl.semaphore_signal(barrier, inc=1, device_id={"col": right}, device_id_type=mesh_ids)
+
+    pl.semaphore_wait(barrier, 1 + jnp.where(col > 0, 1, 0) + jnp.where(col < last, 1, 0))
+
+    def x_copy(piece):
+        return pltpu.make_async_remote_copy(
+            xs.at[0, piece], xs.at[1, piece], x_send.at[piece], x_recv.at[piece],
+            device_id=peer, device_id_type=mesh_ids,
+        )
+
+    def acc_copy(half, chunk):
+        return pltpu.make_async_remote_copy(
+            acc.at[half, chunk], acc.at[half, chunk], acc_send.at[half, chunk], acc_recv.at[half, chunk],
+            device_id={"col": left if half == 0 else right}, device_id_type=mesh_ids,
+        )
+
+    def stage_copy(part):
+        return pltpu.make_async_remote_copy(
+            stage.at[part], gath.at[end_half, part, ctx], stage_send.at[part], stage_recv.at[part],
+            device_id=peer, device_id_type=mesh_ids,
+        )
+
+    def z_copy(half, part, source, target):
+        return pltpu.make_async_remote_copy(
+            gath.at[half, part, source], gath.at[half, part, source],
+            z_send.at[half, part, source], z_recv.at[half, part, source],
+            device_id={"col": target}, device_id_type=mesh_ids,
+        )
+
+    @pl.loop(0, pieces)
+    def _(piece):
+        x_copy(piece).start()
+
+    def filter_block(part, block):
+        mine = lax.rem(block // pieces + ctx, 2)
+        chunk = mine * 2 * pieces + part * pieces + lax.rem(block, pieces)
+        taps = taps_ref.at[part]
+        start = pl.multiple_of(block * rows, rows)
+        scale = scale_ref[pl.ds(start, rows), :]
+
+        @pl.when(block == 0)
+        def _():
+            prev[...] = jnp.zeros_like(prev)
+            gates[0:SUB, :] = jnp.zeros((SUB, width), jnp.float32)
+            shifted[:, rows:, :] = jnp.zeros((SUB, rows, width), jnp.float32)
+
+        shifted[:, 0:rows, :] = shifted[:, rows:, :]
+        filtered = []
+        for which in range(3):
+            now = acc[end_half, chunk, :, which * width : (which + 1) * width].astype(jnp.float32) * scale
+            prev[which, SUB:, :] = now
+            total = taps[3 * which : 3 * which + 1, :] * now
+            for tap in range(1, SHORT_LEN):
+                row = 3 * which + tap
+                total = total + taps[row : row + 1, :] * prev[which, SUB - tap : SUB - tap + rows, :]
+            filtered.append(total)
+            prev[which, 0:SUB, :] = prev[which, rows : rows + SUB, :]
+        gate = filtered[1] * filtered[2]
+        gates[SUB:, :] = gate
+        for move in range(SUB):
+            shifted[move, rows:, :] = gates[SUB - move : SUB - move + rows, :]
+        gates[0:SUB, :] = gates[rows : rows + SUB, :]
+        total = taps[9:10, :] * gate
+        for move in range(SUB):
+            for back in range(0, FILTER_LEN, SUB):
+                row = 16 + back + move
+                total = total + taps[row : row + 1, :] * shifted[move, rows - back : 2 * rows - back, :]
+        value = (filtered[0] * total).astype(jnp.bfloat16)
+        place = pl.ds(pl.multiple_of(lax.rem(block, pieces) * rows, rows), rows)
+
+        @pl.when(mine == 0)
+        def _():
+            gath[end_half, part, ctx, place, :] = value
+
+        @pl.when(mine == 1)
+        def _():
+            stage[part, place, :] = value
+
+    def hand_on(part, first):
+        @pl.when(is_end & (ctx == first))
+        def _():
+            z_copy(end_half, part, ctx, inward).start()
+
+        @pl.when(is_end & (ctx != first))
+        def _():
+            stage_copy(part).start()
+
+    def hand_on_peer(part):
+        @pl.when(is_end)
+        def _():
+            stage_copy(part).wait_recv()
+            z_copy(end_half, part, 1 - ctx, inward).start()
+
+    steps = chunks + 2 * last
+
+    @pl.loop(0, steps)
+    def _(step):
+        first = step - 2 * jnp.minimum(col, last - col)
+
+        @pl.when((first >= 2 * pieces) & (first < 3 * pieces))
+        def _():
+            x_copy(first - 2 * pieces).wait_recv()
+
+        for half in range(2):
+            hops = last - col if half == 0 else col
+            chunk = step - 2 * hops
+
+            @pl.when((chunk >= 0) & (chunk < chunks))
+            def _():
+                part = lax.rem(chunk // pieces, 2)
+                own = lax.dot_general(
+                    xs[chunk // (2 * pieces), lax.rem(chunk, pieces)], w_ref[2 * half + part],
+                    (((1,), (1,)), ((), ())), preferred_element_type=jnp.float32,
+                )
+
+                @pl.when(hops == 0)
+                def _():
+                    acc[half, chunk] = own.astype(jnp.bfloat16)
+
+                @pl.when(hops > 0)
+                def _():
+                    acc_copy(half, chunk).wait_recv()
+                    acc[half, chunk] = (own + acc[half, chunk].astype(jnp.float32)).astype(jnp.bfloat16)
+
+                @pl.when(hops < last)
+                def _():
+                    acc_copy(half, chunk).start()
+
+        @pl.when(is_end & (step >= steps - pieces))
+        def _():
+            @pl.loop(0, 2)
+            def _(more):
+                filter_block(0, 2 * (step - steps + pieces) + more)
+
+    hand_on(0, 0)
+    hand_on(0, 1)
+    for first in range(2):
+        @pl.when(is_end)
+        def _():
+            @pl.loop(first * pieces, (first + 1) * pieces)
+            def _(block):
+                filter_block(1, block)
+
+        if first == 0:
+            hand_on_peer(0)
+        hand_on(1, first)
+    hand_on_peer(1)
+
+    for part in range(2):
+        for turn in range(2):
+            source = ctx if turn == 0 else 1 - ctx
+            for half in range(2):
+                hops = col if half == 0 else last - col
+
+                @pl.when(hops > 0)
+                def _():
+                    z_copy(half, part, source, left).wait_recv()
+
+                @pl.when((hops > 0) & (hops < last))
+                def _():
+                    z_copy(half, part, source, right if half == 0 else left).start()
+
+    for half in range(2):
+        for part in range(2):
+            for source in range(2):
+                place = (half * 2 + part) * 2 + source
+                out_ref[:, place * width : (place + 1) * width] = gath[half, part, source]
+
+    @pl.loop(0, pieces)
+    def _(piece):
+        x_copy(piece).wait_send()
+
+    for half in range(2):
+        @pl.when((last - col if half == 0 else col) < last)
+        def _():
+            @pl.loop(0, chunks)
+            def _(chunk):
+                acc_copy(half, chunk).wait_send()
+
+        @pl.when((col if half == 0 else last - col) < last)
+        def _():
+            for part in range(2):
+                for source in range(2):
+                    z_copy(half, part, source, left).wait_send()
+
+    @pl.when(is_end)
+    def _():
+        for part in range(2):
+            stage_copy(part).wait_send()
+
+
+def chain(last, activations, gain, weights, scale, taps):
+    tokens, features = activations.shape
+    rows = FILTER_LEN
+    pieces = tokens // rows
+    chunks = 4 * pieces
+    width = weights.shape[1] // 3
+    dma = pltpu.SemaphoreType.DMA
+    vmem = pl.BlockSpec(memory_space=pltpu.VMEM)
+    return pl.pallas_call(
+        functools.partial(chain_kernel, last),
+        in_specs=[vmem] * 5,
+        out_specs=vmem,
+        out_shape=jax.ShapeDtypeStruct((tokens, 8 * width), jnp.bfloat16),
+        scratch_shapes=[
+            pltpu.VMEM((2, pieces, rows, features), jnp.bfloat16),
+            pltpu.VMEM((2, chunks, rows, 3 * width), jnp.bfloat16),
+            pltpu.VMEM((3, SUB + rows, width), jnp.float32),
+            pltpu.VMEM((SUB + rows, width), jnp.float32),
+            pltpu.VMEM((SUB, 2 * rows, width), jnp.float32),
+            pltpu.VMEM((2, tokens, width), jnp.bfloat16),
+            pltpu.VMEM((2, 2, 2, tokens, width), jnp.bfloat16),
+            dma((2, chunks)), dma((2, chunks)), dma((pieces,)), dma((pieces,)),
+            dma((2,)), dma((2,)), dma((2, 2, 2)), dma((2, 2, 2)),
+        ],
+        compiler_params=pltpu.CompilerParams(
+            collective_id=0, has_side_effects=True, vmem_limit_bytes=40 * 2**20
+        ),
+    )(activations, gain, weights, scale, taps)
+
+
+def on_device_chain(
+    n_col, activations, norm_gain, w_query, w_key, w_value, short_taps, long_taps, skip_gain, w_out
+):
+    ctx, col = lax.axis_index("ctx"), lax.axis_index("col")
+    tokens, features = activations.shape
+    held = w_query.shape[0]
+    last = n_col - 1
+    width = held // 4
+    group = short_taps.shape[2]
+    weights = jnp.stack([w_query, w_key, w_value]).reshape(3, 4, width, features)
+    weights = jnp.transpose(weights, (1, 0, 2, 3)).reshape(4, 3 * width, features)
+
+    taps = jnp.concatenate(
+        [short_taps.reshape(9, group), skip_gain[None], jnp.zeros((6, group), jnp.float32), long_taps], axis=0
+    )
+    pairs = [(x * n_col + 2 * x + d, x * n_col + d * last) for x in range(2) for d in range(2)]
+    taps = lax.ppermute(taps, ("ctx", "col"), pairs)
+    taps = jnp.transpose(taps.reshape(-1, 2, width), (1, 0, 2))
+
+    w_full = lax.all_gather(w_out, "ctx", axis=0, tiled=True)
+    w_full = jnp.transpose(w_full.reshape(-1, 2, 4, width), (0, 2, 1, 3)).reshape(w_full.shape)
+
+    as_float = activations.astype(jnp.float32)
+    squares = jnp.sum(as_float * as_float, axis=1).reshape(-1, 128)
+    total = squares
+    for step in range(1, n_col):
+        total = total + shift(squares, "col", n_col, step)
+    other = shift(total, "ctx", 2, 1)
+    total = jnp.where(ctx == 0, jnp.concatenate([total, other]), jnp.concatenate([other, total]))
+    scale = lax.rsqrt(total / D + epsilon).reshape(-1, 1)
+
+    block_rows = chain(last, activations, norm_gain[None], weights, scale, taps)
+    out_part = lax.dot_general(
+        block_rows, w_full, (((1,), (1,)), ((), ())), preferred_element_type=jnp.float32
+    )
+    return lax.psum_scatter(out_part.astype(jnp.bfloat16), "row", scatter_dimension=0, tiled=True)
+
+
 def solution(mesh):
     in_specs = (
         P("ctx", "col"),
@@ -138,5 +425,9 @@
         P(("col", "ctx"), "row"),
     )
     out_specs = P(("ctx", "row"), "col")
-    body = functools.partial(on_device, mesh.shape["ctx"], mesh.shape["row"], mesh.shape["col"])
+    n_ctx, n_row, n_col = mesh.shape["ctx"], mesh.shape["row"], mesh.shape["col"]
+    if n_ctx == 2 and n_col == 4:
+        body = functools.partial(on_device_chain, n_col)
+    else:
+        body = functools.partial(on_device, n_ctx, n_row, n_col)
     return jax.shard_map(body, mesh=mesh, in_specs=in_specs, out_specs=out_specs, check_vma=False)

time: 264 us -> 232 us (0.88)
  Pallas kernels: 16.6 us -> 161 us
  waiting for transfers between devices: 157 us -> 32.6 us
  blocking collectives: 32 us -> 0 us
  matrix products: 18.8 us -> 3.68 us
  local copies, waits for them, and re-layouts: 16.4 us -> 10.2 us
    pallas_call x1, Pallas kernels: 16.6 us -> 161 us  [chain(): pl.pallas_call(functools.partial(chain_kernel, last), in_specs=[vmem] * 5...]
    ppermute x4, waiting for transfers between devices: 48.6 us -> 3.52 us  [shift(): lax.ppermute(value, axis, [((i + by) % size, i) for i in range(size)])]
    all_gather x2 -> x1, waiting for transfers between devices: 43.3 us -> 0.01 us  [on_device_chain(): w_full = lax.all_gather(w_out, 'ctx', axis=0, tiled=True)]
    reduce_scatter x3 -> x1, waiting for transfers between devices: 65.4 us -> 29.1 us  [on_device_chain(): lax.psum_scatter(out_part.astype(jnp.bfloat16), 'row', scatter_dimension=...]
    all_gather x1 -> x0, blocking collectives: 20.4 us -> none  [on_device(): taps = lax.all_gather(taps, 'col', axis=1, tiled=True)]
    dot_general x3 -> x1, matrix products: 18.8 us -> 3.68 us  [on_device_chain(): lax.dot_general(block_rows, w_full, (((1,), (1,)), ((), ())), preferred_e...]
    all_to_all x1 -> x0, blocking collectives: 11.7 us -> none  [on_device(): lax.all_to_all(mixed.reshape(n_ctx, tokens, width), 'ctx', split_axis=0,...]
    reshape x4 -> x1, local copies, waits for them, and re-layouts: 3.3 us -> 0.01 us  [on_device_chain(): short_taps.reshape(9, group)]
  transfers between devices with their start and end apart: 9 -> 7, of which waited for: 6 -> 3; matrix products, arithmetic and copies ran while one was open for 7% -> 2% of each run, Pallas kernels for 6% -> 69%
where the time goes in v2:
time: 232 us
  Pallas kernels  161 us (69%)
  waiting for transfers between devices  32.6 us (14%)
  between operations  13.5 us (6%)
  local copies, waits for them, and re-layouts  10.2 us (4%)
  starting transfers between devices  8.32 us (4%)
  matrix products  3.68 us (2%)
  other arithmetic  2.78 us (1%)
    pallas_call x1, Pallas kernels, chain(): pl.pallas_call(functools.partial(chain_kernel, last), in_specs=[vmem] * 5...  161 us
    reduce_scatter x1, waiting for transfers between devices, on_device_chain(): lax.psum_scatter(out_part.astype(jnp.bfloat16), 'row', scatter_dimension=...  29.1 us
    ppermute x4, starting transfers between devices, shift(): lax.ppermute(value, axis, [((i + by) % size, i) for i in range(size)])  7.61 us
    unnamed x19, local copies, waits for them, and re-layouts  6.88 us
  transfers between devices with their start and end apart: 7, of which 3 were waited for; matrix products, arithmetic and copies ran while one was open for 2% of the time, Pallas kernels for 69%

profile of v2, /device:TPU:0, one launch (start us, length us, event | category | flops | bytes accessed | tf_op | source)
XLA Modules:
  0.0 231.7 jit_solution(13476409977950034702)
XLA Ops:
  6.5 2.4 %copy.23 = bf16[512,1024]{0,1:T(8,128)(2,1)} copy(bf16[512,1024]{1,0:T(8,128)(2,1)} %param.17) | data formatting | bytes 2097152 | tf_op args[8]
  9.0 0.0 all-gather.2.cloned.1.call-update
  9.0 0.0 reduce-scatter.2.cloned.1.call-start
  9.1 0.5 multiply_reduce_fusion
  9.5 5.1 %collective-permute-start = (f32[8,128]{1,0:T(8,128)S(1)}, f32[8,128]{1,0:T(8,128)S(1)}, u32[]{:S(2)}, u32[]{:S(2)}) collective-permute-start(f32[8,128]{1,0:T(8,128)S(1)} %bitcast.38), channel_id=1, source_target_pairs={{1,0},{2,1},{3,2},{0,3},{5,4},{6,5},{7,6},{4,7},{9,8},{10,9},{11,1... | collective-permute-start | bytes 12296 | tf_op jit(solution)/shard_map/ppermute | solution.py:78
  14.6 1.0 collective-permute-start.2
  15.7 0.1 pad.2.clone
  15.8 0.1 pad_maximum_fusion.1
  15.8 0.7 collective-permute-start.4
  16.5 2.6 %collective-permute-done.1 = f32[8,128]{1,0:T(8,128)S(1)} collective-permute-done((f32[8,128]{1,0:T(8,128)S(1)}, f32[8,128]{1,0:T(8,128)S(1)}, u32[]{:S(2)}, u32[]{:S(2)}) %collective-permute-start.1) | collective-permute-done | bytes 4128 | tf_op jit(solution)/shard_map/ppermute | solution.py:78
  19.1 0.9 collective-permute-done.2
  20.1 1.5 collective-permute-start.3
  21.5 2.2 pad_maximum_fusion
  23.8 1.3 copy.22.scale_ref
  25.2 0.0 copy-start.1
  25.2 1.6 copy-done.1
  26.8 1.2 copy-done.2
  28.0 160.5 %shard_map.91 = bf16[1024,1024]{1,0:T(8,128)(2,1)S(1)} custom-call(bf16[1024,1024]{1,0:T(8,128)(2,1)S(1)} %copy-done.1, f32[1,1024]{1,0:T(1,128)S(1)} %bitcast.31, bf16[4,384,1024]{2,1,0:T(8,128)(2,1)S(1)} %bitcast.30, f32[2048,1]{1,0:T(8,128)S(1)} %copy-done.2, f32[2,144,128]{2,1,0:T(8,128)S(1)} %bitcast_bitcast_fusion.taps_ref), custom_call_target="tpu_custom_call" | custom-call | tf_op jit(solution)/shard_map/pallas_call | solution.py:355
  188.5 1.3 copy-done.3
  189.9 1.9 copy.24
  191.8 0.3 copy-done.4
  192.1 3.7 %convolution_convert_fusion = bf16[1024,1024]{1,0:T(8,128)(2,1)} fusion(bf16[1024,1024]{1,0:T(8,128)(2,1)S(1)} %copy-done.4, bf16[1024,1024]{0,1:T(8,128)(2,1)S(1)} %bitcast.33), kind=kOutput, calls=%fused_computation.2 | convolution fusion | flops 2148532224 | bytes 6291456 | tf_op jit(solution)/shard_map/dot_general | solution.py:409
  195.8 0.0 reduce-scatter.2.cloned.1.call-update
  195.8 29.1 %reduce-scatter.2.cloned.1.call-done = bf16[256,1024]{1,0:T(8,128)(2,1)} async-done(((bf16[1024,1024]{1,0:T(8,128)(2,1)}), bf16[256,1024]{1,0:T(8,128)(2,1)}) %reduce-scatter.2.cloned.1.call-update) | async-done | bytes 524304 | tf_op jit(solution)/shard_map/reduce_scatter | solution.py:412
  (24 shorter events, 0.1 us)
Async XLA Ops:
  6.5 2.5 %copy-start = (bf16[1024,1024]{1,0:T(8,128)(2,1)S(1)}, bf16[1024,1024]{1,0:T(8,128)(2,1)}, u32[]{:S(2)}) copy-start(bf16[1024,1024]{1,0:T(8,128)(2,1)} %x_ref.1) | copy-start | bytes 6291460
  6.5 183.3 %all-gather.2.cloned.1.call-start = ((), (), s32[]{:S(2)}) async-start(), calls=%async_computation.1 | async-start | bytes 3145728 | tf_op jit(solution)/shard_map/all_gather | solution.py:396
  9.0 6.7 %copy-start.7 = (f32[3,3,256]{2,1,0:T(4,128)S(1)}, f32[3,3,256]{2,1,0:T(4,128)}, u32[]{:S(2)}) copy-start(f32[3,3,256]{2,1,0:T(4,128)} %param.14) | copy-start | bytes 27652
  9.0 6.8 %copy-start.6 = (f32[128,256]{1,0:T(8,128)S(1)}, f32[128,256]{1,0:T(8,128)}, u32[]{:S(2)}) copy-start(f32[128,256]{1,0:T(8,128)} %param.15) | copy-start | bytes 393220
  9.0 6.8 %copy-start.8 = (f32[256]{0:T(256)S(1)}, f32[256]{0:T(256)}, u32[]{:S(2)}) copy-start(f32[256]{0:T(256)} %param.16) | copy-start | bytes 3076
  9.0 215.8 %reduce-scatter.2.cloned.1.call-start = ((), (), s32[]{:S(2)}) async-start(), calls=%async_computation.2 | async-start | bytes 2621440 | tf_op jit(solution)/shard_map/reduce_scatter | solution.py:412
  9.5 7.0 %collective-permute-start = (f32[8,128]{1,0:T(8,128)S(1)}, f32[8,128]{1,0:T(8,128)S(1)}, u32[]{:S(2)}, u32[]{:S(2)}) collective-permute-start(f32[8,128]{1,0:T(8,128)S(1)} %bitcast.38), channel_id=1, source_target_pairs={{1,0},{2,1},{3,2},{0,3},{5,4},{6,5},{7,6},{4,7},{9,8},{10,9},{11,1... | collective-permute-start | bytes 12296 | tf_op jit(solution)/shard_map/ppermute | solution.py:78
  14.6 4.5 %collective-permute-start.1 = (f32[8,128]{1,0:T(8,128)S(1)}, f32[8,128]{1,0:T(8,128)S(1)}, u32[]{:S(2)}, u32[]{:S(2)}) collective-permute-start(f32[8,128]{1,0:T(8,128)S(1)} %bitcast.39), channel_id=1, source_target_pairs={{2,0},{3,1},{0,2},{1,3},{6,4},{7,5},{4,6},{5,7},{10,8},{11,9},{8,1... | collective-permute-start | bytes 12296 | tf_op jit(solution)/shard_map/ppermute | solution.py:78
  14.6 5.4 %collective-permute-start.2 = (f32[8,128]{1,0:T(8,128)S(1)}, f32[8,128]{1,0:T(8,128)S(1)}, u32[]{:S(2)}, u32[]{:S(2)}) collective-permute-start(f32[8,128]{1,0:T(8,128)S(1)} %bitcast.40), channel_id=1, source_target_pairs={{3,0},{0,1},{1,2},{2,3},{7,4},{4,5},{5,6},{6,7},{11,8},{8,9},{9,10... | collective-permute-start | bytes 12296 | tf_op jit(solution)/shard_map/ppermute | solution.py:78
  15.8 9.3 %collective-permute-start.4 = (f32[144,256]{1,0:T(8,128)S(1)}, f32[144,256]{1,0:T(8,128)S(1)}, u32[]{:S(2)}, u32[]{:S(2)}) collective-permute-start(f32[144,256]{1,0:T(8,128)S(1)} %pad_maximum_fusion.1), channel_id=1, source_target_pairs={{0,0},{1,3},{18,16},{19,19},{4,4},{5,7},{22,20},{23,23},{8,8},{9,1... | collective-permute-start | bytes 442376 | tf_op jit(solution)/shard_map/ppermute | solution.py:393
  20.1 3.7 %collective-permute-start.3 = (f32[8,128]{1,0:T(8,128)S(1)}, f32[8,128]{1,0:T(8,128)S(1)}, u32[]{:S(2)}, u32[]{:S(2)}) collective-permute-start(f32[8,128]{1,0:T(8,128)S(1)} %add_add_fusion), channel_id=1, source_target_pairs={{16,0},{0,16},{17,1},{1,17},{18,2},{2,18},{19,3},{3,19},{20,4},{4,... | collective-permute-start | bytes 12296 | tf_op jit(solution)/shard_map/ppermute | solution.py:78
  21.5 3.6 %copy-start.5 = (f32[1024]{0:T(1024)S(1)}, f32[1024]{0:T(1024)}, u32[]{:S(2)}) copy-start(f32[1024]{0:T(1024)} %param.10) | copy-start | bytes 12292
  25.2 1.6 copy-start.1
  26.8 1.2 copy-start.2
  188.5 1.3 copy-start.3
  189.9 2.2 copy-start.4
Sparse Core Ops, SparseCore 0:
  9.1 50.4 all-gather.1
  195.9 28.8 reduce-scatter.1

commit v3 on v2

--- a/solution.py
+++ b/solution.py
@@ -125,9 +125,13 @@
     return lax.psum_scatter(out_part.astype(jnp.bfloat16), "row", scatter_dimension=0, tiled=True)
 
 
+QUARTERS = 4
+
+
 def chain_kernel(
-    last, x_ref, gain_ref, w_ref, scale_ref, taps_ref, out_ref,
-    xs, acc, prev, gates, shifted, stage, gath,
+    last, x_ref, gain_ref, wq_ref, wk_ref, wv_ref, squares_ref, own_taps, out_ref,
+    xs, w_ref, acc, taps_ref, totals, prev, gates, shifted, stage, gath,
+    w_sem, taps_send, taps_recv, sq_send, sq_recv,
     acc_send, acc_recv, x_send, x_recv, stage_send, stage_recv, z_send, z_recv,
 ):
     ctx, col = lax.axis_index("ctx"), lax.axis_index("col")
@@ -135,27 +139,35 @@
     chunks = acc.shape[1]
     rows = xs.shape[2]
     width = gath.shape[4]
+    quarter = gath.shape[3] // QUARTERS
+    per = pieces // QUARTERS
+    n_col = last + 1
     is_end = (col == 0) | (col == last)
     end_half = jnp.where(col == 0, 0, 1)
-    inward = jnp.where(col == 0, 1, last - 1)
     left, right = jnp.maximum(col - 1, 0), jnp.minimum(col + 1, last)
     peer = {"ctx": 1 - ctx}
     mesh_ids = pl.DeviceIdType.MESH
 
+    def w_copy(group, which):
+        source = (wq_ref, wk_ref, wv_ref)[which]
+        return pltpu.make_async_copy(
+            source.at[pl.ds(group * width, width)], w_ref.at[group, pl.ds(which * width, width)],
+            w_sem.at[group, which],
+        )
+
+    for group in range(4):
+        for which in range(3):
+            w_copy(group, which).start()
+
+    barrier = pltpu.get_barrier_semaphore()
+    for far in range(2):
+        for away in range(n_col):
+            if far or away:
+                other = {"ctx": lax.rem(ctx + far, 2), "col": lax.rem(col + away, n_col)}
+                pl.semaphore_signal(barrier, inc=1, device_id=other, device_id_type=mesh_ids)
+
     xs[0] = (x_ref[...].astype(jnp.float32) * gain_ref[...]).astype(jnp.bfloat16).reshape(xs.shape[1:])
-
-    barrier = pltpu.get_barrier_semaphore()
-    pl.semaphore_signal(barrier, inc=1, device_id=peer, device_id_type=mesh_ids)
-
-    @pl.when(col > 0)
-    def _():
-        pl.semaphore_signal(barrier, inc=1, device_id={"col": left}, device_id_type=mesh_ids)
-
-    @pl.when(col < last)
-    def _():
-        pl.semaphore_signal(barrier, inc=1, device_id={"col": right}, device_id_type=mesh_ids)
-
-    pl.semaphore_wait(barrier, 1 + jnp.where(col > 0, 1, 0) + jnp.where(col < last, 1, 0))
+    pl.semaphore_wait(barrier, 2 * n_col - 1)
 
     def x_copy(piece):
         return pltpu.make_async_remote_copy(
@@ -169,86 +181,145 @@
             device_id={"col": left if half == 0 else right}, device_id_type=mesh_ids,
         )
 
-    def stage_copy(part):
+    def stage_copy(part, place):
+        rows_of = pl.ds(pl.multiple_of(place * quarter, quarter), quarter)
         return pltpu.make_async_remote_copy(
-            stage.at[part], gath.at[end_half, part, ctx], stage_send.at[part], stage_recv.at[part],
+            stage.at[part, rows_of], gath.at[end_half, part, ctx, rows_of],
+            stage_send.at[part, place], stage_recv.at[part, place],
             device_id=peer, device_id_type=mesh_ids,
         )
 
-    def z_copy(half, part, source, target):
+    def z_copy(half, part, source, place):
+        rows_of = pl.ds(pl.multiple_of(place * quarter, quarter), quarter)
         return pltpu.make_async_remote_copy(
-            gath.at[half, part, source], gath.at[half, part, source],
-            z_send.at[half, part, source], z_recv.at[half, part, source],
-            device_id={"col": target}, device_id_type=mesh_ids,
+            gath.at[half, part, source, rows_of], gath.at[half, part, source, rows_of],
+            z_send.at[half, part, source, place], z_recv.at[half, part, source, place],
+            device_id={"col": right if half == 0 else left}, device_id_type=mesh_ids,
         )
+
+    def sq_copy(far, away):
+        me = ctx * n_col + col
+        return pltpu.make_async_remote_copy(
+            squares_ref, totals.at[me], sq_send.at[far, 0 if away == 0 else 1], sq_recv.at[me],
+            device_id={"ctx": lax.rem(ctx + far, 2), "col": away}, device_id_type=mesh_ids,
+        )
+
+    taps_owner = col // 2 == ctx
+    taps_end = lax.rem(col, 2) * last
+    taps_copy = pltpu.make_async_remote_copy(
+        own_taps, taps_ref, taps_send, taps_recv, device_id={"col": taps_end}, device_id_type=mesh_ids
+    )
 
     @pl.loop(0, pieces)
     def _(piece):
         x_copy(piece).start()
 
-    def filter_block(part, block):
-        mine = lax.rem(block // pieces + ctx, 2)
-        chunk = mine * 2 * pieces + part * pieces + lax.rem(block, pieces)
+    for far in range(2):
+        for away in (0, last):
+            @pl.when((col != away) if far == 0 else (col >= 0))
+            def _():
+                sq_copy(far, away).start()
+
+    @pl.when(taps_owner & (taps_end != col))
+    def _():
+        taps_copy.start()
+
+    @pl.when(taps_owner & (taps_end == col))
+    def _():
+        taps_ref[...] = own_taps[...]
+
+    @pl.when(is_end)
+    def _():
+        totals[ctx * n_col + col] = squares_ref[...]
+
+    for group in range(4):
+        for which in range(3):
+            w_copy(group, which).wait()
+
+    def wait_small():
+        for source in range(2 * n_col):
+            @pl.when(source != ctx * n_col + col)
+            def _():
+                pltpu.make_async_remote_copy(
+                    squares_ref, totals.at[source], sq_send.at[0, 0], sq_recv.at[source],
+                    device_id=peer, device_id_type=mesh_ids,
+                ).wait_recv()
+
+        @pl.when(jnp.logical_not(taps_owner & (taps_end == col)))
+        def _():
+            taps_copy.wait_recv()
+
+        for half in range(2):
+            total = totals[half * n_col]
+            for source in range(1, n_col):
+                total = total + totals[half * n_col + source]
+            totals[half * n_col] = lax.rsqrt(total / D + epsilon)
+
+    diagonal = lax.broadcasted_iota(jnp.int32, (rows, rows), 0) == lax.broadcasted_iota(
+        jnp.int32, (rows, rows), 1
+    )
+
+    def filter_block(part, mine, place, again):
+        chunk = mine * 2 * pieces + part * pieces + place
+        half = lax.rem(ctx + mine, 2)
+        row_scale = totals[half * n_col, pl.ds(place, 1), :]
+        scale = jnp.sum(jnp.where(diagonal, row_scale, 0.0), axis=1, keepdims=True)
         taps = taps_ref.at[part]
-        start = pl.multiple_of(block * rows, rows)
-        scale = scale_ref[pl.ds(start, rows), :]
-
-        @pl.when(block == 0)
-        def _():
-            prev[...] = jnp.zeros_like(prev)
-            gates[0:SUB, :] = jnp.zeros((SUB, width), jnp.float32)
-            shifted[:, rows:, :] = jnp.zeros((SUB, rows, width), jnp.float32)
-
-        shifted[:, 0:rows, :] = shifted[:, rows:, :]
+
+        if not again:
+            @pl.when((place == 0) & ((mine == 0) | (ctx == 1)))
+            def _():
+                prev[part] = jnp.zeros(prev.shape[1:], jnp.float32)
+                gates[part, 0:SUB, :] = jnp.zeros((SUB, width), jnp.float32)
+                shifted[part, :, rows:, :] = jnp.zeros((SUB, rows, width), jnp.float32)
+
+        shifted[part, :, 0:rows, :] = shifted[part, :, rows:, :]
         filtered = []
         for which in range(3):
             now = acc[end_half, chunk, :, which * width : (which + 1) * width].astype(jnp.float32) * scale
-            prev[which, SUB:, :] = now
+            prev[part, which, SUB:, :] = now
             total = taps[3 * which : 3 * which + 1, :] * now
             for tap in range(1, SHORT_LEN):
                 row = 3 * which + tap
-                total = total + taps[row : row + 1, :] * prev[which, SUB - tap : SUB - tap + rows, :]
+                total = total + taps[row : row + 1, :] * prev[part, which, SUB - tap : SUB - tap + rows, :]
             filtered.append(total)
-            prev[which, 0:SUB, :] = prev[which, rows : rows + SUB, :]
+            prev[part, which, 0:SUB, :] = prev[part, which, rows : rows + SUB, :]
         gate = filtered[1] * filtered[2]
-        gates[SUB:, :] = gate
+        gates[part, SUB:, :] = gate
         for move in range(SUB):
-            shifted[move, rows:, :] = gates[SUB - move : SUB - move + rows, :]
-        gates[0:SUB, :] = gates[rows : rows + SUB, :]
+            shifted[part, move, rows:, :] = gates[part, SUB - move : SUB - move + rows, :]
+        gates[part, 0:SUB, :] = gates[part, rows : rows + SUB, :]
         total = taps[9:10, :] * gate
         for move in range(SUB):
             for back in range(0, FILTER_LEN, SUB):
                 row = 16 + back + move
-                total = total + taps[row : row + 1, :] * shifted[move, rows - back : 2 * rows - back, :]
+                total = total + taps[row : row + 1, :] * shifted[part, move, rows - back : 2 * rows - back, :]
         value = (filtered[0] * total).astype(jnp.bfloat16)
-        place = pl.ds(pl.multiple_of(lax.rem(block, pieces) * rows, rows), rows)
+        spot = pl.ds(pl.multiple_of(place * rows, rows), rows)
 
         @pl.when(mine == 0)
         def _():
-            gath[end_half, part, ctx, place, :] = value
+            gath[end_half, part, ctx, spot, :] = value
 
         @pl.when(mine == 1)
         def _():
-            stage[part, place, :] = value
-
-    def hand_on(part, first):
-        @pl.when(is_end & (ctx == first))
-        def _():
-            z_copy(end_half, part, ctx, inward).start()
-
-        @pl.when(is_end & (ctx != first))
-        def _():
-            stage_copy(part).start()
-
-    def hand_on_peer(part):
-        @pl.when(is_end)
-        def _():
-            stage_copy(part).wait_recv()
-            z_copy(end_half, part, 1 - ctx, inward).start()
-
-    steps = chunks + 2 * last
-
-    @pl.loop(0, steps)
+            stage[part, spot, :] = value
+
+    def pass_on(half, hops, part, source, place, from_peer):
+        @pl.when(hops > 0)
+        def _():
+            z_copy(half, part, source, place).wait_recv()
+
+        if from_peer:
+            @pl.when(hops == 0)
+            def _():
+                stage_copy(part, place).wait_recv()
+
+        @pl.when(hops < last)
+        def _():
+            z_copy(half, part, source, place).start()
+
+    @pl.loop(0, chunks + 4 * last)
     def _(step):
         first = step - 2 * jnp.minimum(col, last - col)
 
@@ -281,39 +352,55 @@
                 def _():
                     acc_copy(half, chunk).start()
 
-        @pl.when(is_end & (step >= steps - pieces))
-        def _():
-            @pl.loop(0, 2)
-            def _(more):
-                filter_block(0, 2 * (step - steps + pieces) + more)
-
-    hand_on(0, 0)
-    hand_on(0, 1)
-    for first in range(2):
-        @pl.when(is_end)
-        def _():
-            @pl.loop(first * pieces, (first + 1) * pieces)
-            def _(block):
-                filter_block(1, block)
-
-        if first == 0:
-            hand_on_peer(0)
-        hand_on(1, first)
-    hand_on_peer(1)
-
-    for part in range(2):
-        for turn in range(2):
-            source = ctx if turn == 0 else 1 - ctx
-            for half in range(2):
-                hops = col if half == 0 else last - col
-
-                @pl.when(hops > 0)
+        done = step - 2 * last
+
+        @pl.when(is_end & (done == 0))
+        def _():
+            wait_small()
+
+        @pl.when(is_end & (done >= 0) & (done < chunks))
+        def _():
+            mine, part, place = done // (2 * pieces), lax.rem(done // pieces, 2), lax.rem(done, pieces)
+            filter_block(part, mine, place, False)
+
+            @pl.when((mine == 1) & (lax.rem(place, per) == per - 1))
+            def _():
+                stage_copy(part, place // per).start()
+
+            @pl.when((mine == 1) & (place == pieces - 1) & (ctx == 1))
+            def _():
+                filter_block(part, 0, 0, True)
+
+        for half in range(2):
+            hops = col if half == 0 else last - col
+            event = step - 2 * last - 2 * hops
+            full = lax.rem(event + per, per) == per - 1
+            index = event // per
+
+            @pl.when((event >= 0) & (event < 2 * pieces) & full)
+            def _():
+                place = lax.rem(index, QUARTERS)
+
+                @pl.when((ctx == 0) | (place > 0))
                 def _():
-                    z_copy(half, part, source, left).wait_recv()
-
-                @pl.when((hops > 0) & (hops < last))
-                def _():
-                    z_copy(half, part, source, right if half == 0 else left).start()
+                    pass_on(half, hops, index // QUARTERS, ctx, place, False)
+
+            @pl.when((event >= 2 * pieces + per) & (event < chunks) & full)
+            def _():
+                late = index - 2 * QUARTERS - 1
+                pass_on(half, hops, late // QUARTERS, 1 - ctx, lax.rem(late, QUARTERS), True)
+
+            @pl.when((event == 3 * pieces) & (ctx == 1))
+            def _():
+                pass_on(half, hops, 0, ctx, 0, False)
+
+    for half in range(2):
+        hops = col if half == 0 else last - col
+        @pl.when(ctx == 1)
+        def _():
+            pass_on(half, hops, 1, ctx, 0, False)
+
+        pass_on(half, hops, 1, 1 - ctx, QUARTERS - 1, True)
 
     for half in range(2):
         for part in range(2):
@@ -325,6 +412,16 @@
     def _(piece):
         x_copy(piece).wait_send()
 
+    for far in range(2):
+        for away in (0, last):
+            @pl.when((col != away) if far == 0 else (col >= 0))
+            def _():
+                sq_copy(far, away).wait_send()
+
+    @pl.when(taps_owner & (taps_end != col))
+    def _():
+        taps_copy.wait_send()
+
     for half in range(2):
         @pl.when((last - col if half == 0 else col) < last)
         def _():
@@ -336,76 +433,70 @@
         def _():
             for part in range(2):
                 for source in range(2):
-                    z_copy(half, part, source, left).wait_send()
+                    for place in range(QUARTERS):
+                        z_copy(half, part, source, place).wait_send()
 
     @pl.when(is_end)
     def _():
         for part in range(2):
-            stage_copy(part).wait_send()
-
-
-def chain(last, activations, gain, weights, scale, taps):
+            for place in range(QUARTERS):
+                stage_copy(part, place).wait_send()
+
+
+def chain(last, activations, gain, weights, squares, taps):
     tokens, features = activations.shape
     rows = FILTER_LEN
     pieces = tokens // rows
     chunks = 4 * pieces
-    width = weights.shape[1] // 3
+    width = weights[0].shape[0] // 4
     dma = pltpu.SemaphoreType.DMA
     vmem = pl.BlockSpec(memory_space=pltpu.VMEM)
+    hbm = pl.BlockSpec(memory_space=pl.ANY)
     return pl.pallas_call(
         functools.partial(chain_kernel, last),
-        in_specs=[vmem] * 5,
+        in_specs=[vmem, vmem, hbm, hbm, hbm, vmem, vmem],
         out_specs=vmem,
         out_shape=jax.ShapeDtypeStruct((tokens, 8 * width), jnp.bfloat16),
         scratch_shapes=[
             pltpu.VMEM((2, pieces, rows, features), jnp.bfloat16),
+            pltpu.VMEM((4, 3 * width, features), jnp.bfloat16),
             pltpu.VMEM((2, chunks, rows, 3 * width), jnp.bfloat16),
-            pltpu.VMEM((3, SUB + rows, width), jnp.float32),
-            pltpu.VMEM((SUB + rows, width), jnp.float32),
-            pltpu.VMEM((SUB, 2 * rows, width), jnp.float32),
+            pltpu.VMEM(taps.shape, jnp.float32),
+            pltpu.VMEM((2 * (last + 1),) + squares.shape, jnp.float32),
+            pltpu.VMEM((2, 3, SUB + rows, width), jnp.float32),
+            pltpu.VMEM((2, SUB + rows, width), jnp.float32),
+            pltpu.VMEM((2, SUB, 2 * rows, width), jnp.float32),
             pltpu.VMEM((2, tokens, width), jnp.bfloat16),
             pltpu.VMEM((2, 2, 2, tokens, width), jnp.bfloat16),
+            dma((4, 3)), dma, dma, dma((2, 2)), dma((2 * (last + 1),)),
             dma((2, chunks)), dma((2, chunks)), dma((pieces,)), dma((pieces,)),
-            dma((2,)), dma((2,)), dma((2, 2, 2)), dma((2, 2, 2)),
+            dma((2, QUARTERS)), dma((2, QUARTERS)), dma((2, 2, 2, QUARTERS)), dma((2, 2, 2, QUARTERS)),
         ],
         compiler_params=pltpu.CompilerParams(
-            collective_id=0, has_side_effects=True, vmem_limit_bytes=40 * 2**20
+            collective_id=0, has_side_effects=True, vmem_limit_bytes=44 * 2**20
         ),
-    )(activations, gain, weights, scale, taps)
+    )(activations, gain, *weights, squares, taps)
 
 
 def on_device_chain(
     n_col, activations, norm_gain, w_query, w_key, w_value, short_taps, long_taps, skip_gain, w_out
 ):
-    ctx, col = lax.axis_index("ctx"), lax.axis_index("col")
-    tokens, features = activations.shape
     held = w_query.shape[0]
-    last = n_col - 1
     width = held // 4
     group = short_taps.shape[2]
-    weights = jnp.stack([w_query, w_key, w_value]).reshape(3, 4, width, features)
-    weights = jnp.transpose(weights, (1, 0, 2, 3)).reshape(4, 3 * width, features)
 
     taps = jnp.concatenate(
         [short_taps.reshape(9, group), skip_gain[None], jnp.zeros((6, group), jnp.float32), long_taps], axis=0
     )
-    pairs = [(x * n_col + 2 * x + d, x * n_col + d * last) for x in range(2) for d in range(2)]
-    taps = lax.ppermute(taps, ("ctx", "col"), pairs)
     taps = jnp.transpose(taps.reshape(-1, 2, width), (1, 0, 2))
 
     w_full = lax.all_gather(w_out, "ctx", axis=0, tiled=True)
     w_full = jnp.transpose(w_full.reshape(-1, 2, 4, width), (0, 2, 1, 3)).reshape(w_full.shape)
 
     as_float = activations.astype(jnp.float32)
-    squares = jnp.sum(as_float * as_float, axis=1).reshape(-1, 128)
-    total = squares
-    for step in range(1, n_col):
-        total = total + shift(squares, "col", n_col, step)
-    other = shift(total, "ctx", 2, 1)
-    total = jnp.where(ctx == 0, jnp.concatenate([total, other]), jnp.concatenate([other, total]))
-    scale = lax.rsqrt(total / D + epsilon).reshape(-1, 1)
-
-    block_rows = chain(last, activations, norm_gain[None], weights, scale, taps)
+    squares = jnp.sum(as_float * as_float, axis=1).reshape(-1, FILTER_LEN)
+
+    block_rows = chain(n_col - 1, activations, norm_gain[None], (w_query, w_key, w_value), squares, taps)
     out_part = lax.dot_general(
         block_rows, w_full, (((1,), (1,)), ((), ())), preferred_element_type=jnp.float32
     )

time: 232 us -> 247 us (1.065)
  Pallas kernels: 161 us -> 190 us
  starting transfers between devices: 8.32 us -> 0.08 us
  local copies, waits for them, and re-layouts: 10.2 us -> 7.21 us
    pallas_call x1, Pallas kernels: 161 us -> 190 us  [chain(): pl.pallas_call(functools.partial(chain_kernel, last), in_specs=[vmem, vme...]
    ppermute x5 -> x0, starting transfers between devices: 8.28 us -> none  [the longest x4 7.61 us: shift(): lax.ppermute(value, axis, [((i + by) % size, i) for i in range(size)])]
    ppermute x5 -> x0, waiting for transfers between devices: 3.52 us -> none  [the longest x4 3.52 us: shift(): lax.ppermute(value, axis, [((i + by) % size, i) for i in range(size)])]
    unnamed x19 -> x22, local copies, waits for them, and re-layouts: 6.88 us -> 5.1 us
  transfers between devices with their start and end apart: 7 -> 2, of which waited for: 3 -> 1; matrix products, arithmetic and copies ran while one was open for 2% -> 0% of each run, Pallas kernels for 69% -> 77%
where the time goes in v3:
time: 247 us; the launch traced here: 246 us
  Pallas kernels  190 us (77%)
  waiting for transfers between devices  31.3 us (13%)
  between operations  13.5 us (5%)
  local copies, waits for them, and re-layouts  7.21 us (3%)
  matrix products  3.68 us (1%)
    pallas_call x1, Pallas kernels, chain(): pl.pallas_call(functools.partial(chain_kernel, last), in_specs=[vmem, vme...  190 us
    reduce_scatter x1, waiting for transfers between devices, on_device_chain(): lax.psum_scatter(out_part.astype(jnp.bfloat16), 'row', scatter_dimension=...  31.2 us
    unnamed x22, local copies, waits for them, and re-layouts  5.1 us
  transfers between devices with their start and end apart: 2, of which 1 were waited for; matrix products, arithmetic and copies ran while one was open for 0% of the time, Pallas kernels for 77%

profile of v3, /device:TPU:0, one launch (start us, length us, event | category | flops | bytes accessed | tf_op | source)
XLA Modules:
  0.0 246.4 jit_solution(12854450821939002704)
XLA Ops:
  6.5 0.0 all-gather.2.cloned.1.call-start
  6.6 2.4 copy.16
  9.0 0.0 all-gather.2.cloned.1.call-update
  9.0 0.0 reduce-scatter.2.cloned.1.call-start
  9.1 0.1 copy.13
  9.2 0.1 copy.15
  9.3 0.0 copy-start.4
  9.4 0.0 copy-start.5
  9.4 0.1 pad.2.clone
  9.5 0.0 copy-done.9
  9.5 0.1 maximum_bitcast_fusion.own_taps
  9.6 0.0 copy-done
  9.6 0.5 multiply_reduce_fusion
  10.0 0.2 copy-done.3
  10.2 0.0 copy-done.6
  10.2 0.4 copy-done.4
  10.7 0.3 copy-done.5
  11.0 190.1 %shard_map.91 = bf16[1024,1024]{1,0:T(8,128)(2,1)S(1)} custom-call(bf16[1024,1024]{1,0:T(8,128)(2,1)S(1)} %copy-done, f32[1,1024]{1,0:T(1,128)S(1)} %bitcast.13, bf16[512,1024]{1,0:T(8,128)(2,1)S(1)} %copy-done.3, bf16[512,1024]{1,0:T(8,128)(2,1)S(1)} %copy-done.4, bf16[512,1024]{1,0:T(8,128)(2,1)S(1)} %copy-done.5, f32[8,128]{1,0:T(8,128)S(1)} %bitcast.12, ...), custom_call_target="tpu_custom_call" | custom-call | tf_op jit(solution)/shard_map/pallas_call | solution.py:455
  201.1 1.3 copy-done.1
  202.4 1.9 copy.17
  204.3 0.3 copy-done.2
  204.6 3.7 %convolution_convert_fusion = bf16[1024,1024]{1,0:T(8,128)(2,1)} fusion(bf16[1024,1024]{1,0:T(8,128)(2,1)S(1)} %copy-done.2, bf16[1024,1024]{0,1:T(8,128)(2,1)S(1)} %bitcast.15), kind=kOutput, calls=%fused_computation.1 | convolution fusion | flops 2148532224 | bytes 6291456 | tf_op jit(solution)/shard_map/dot_general | solution.py:500
  208.3 0.0 reduce-scatter.2.cloned.1.call-update
  208.3 31.2 %reduce-scatter.2.cloned.1.call-done = bf16[256,1024]{1,0:T(8,128)(2,1)} async-done(((bf16[1024,1024]{1,0:T(8,128)(2,1)}), bf16[256,1024]{1,0:T(8,128)(2,1)}) %reduce-scatter.2.cloned.1.call-update) | async-done | bytes 524304 | tf_op jit(solution)/shard_map/reduce_scatter | solution.py:503
  (14 shorter events, 0.0 us)
Async XLA Ops:
  6.5 2.6 %copy-start.8 = (f32[3,3,256]{2,1,0:T(4,128)S(1)}, f32[3,3,256]{2,1,0:T(4,128)}, u32[]{:S(2)}) copy-start(f32[3,3,256]{2,1,0:T(4,128)} %param.14) | copy-start | bytes 27652
  6.5 2.6 %copy-start.7 = (f32[128,256]{1,0:T(8,128)S(1)}, f32[128,256]{1,0:T(8,128)}, u32[]{:S(2)}) copy-start(f32[128,256]{1,0:T(8,128)} %param.15) | copy-start | bytes 393220
  6.5 2.9 %copy-start.9 = (f32[256]{0:T(256)S(1)}, f32[256]{0:T(256)}, u32[]{:S(2)}) copy-start(f32[256]{0:T(256)} %param.16) | copy-start | bytes 3076
  6.5 3.0 %copy-start = (bf16[1024,1024]{1,0:T(8,128)(2,1)S(1)}, bf16[1024,1024]{1,0:T(8,128)(2,1)}, u32[]{:S(2)}) copy-start(bf16[1024,1024]{1,0:T(8,128)(2,1)} %x_ref.1) | copy-start | bytes 6291460
  6.5 195.8 %all-gather.2.cloned.1.call-start = ((), (), s32[]{:S(2)}) async-start(), calls=%async_computation.1 | async-start | bytes 3145728 | tf_op jit(solution)/shard_map/all_gather | solution.py:493
  9.0 1.2 copy-start.3
  9.0 1.2 copy-start.6
  9.0 230.5 %reduce-scatter.2.cloned.1.call-start = ((), (), s32[]{:S(2)}) async-start(), calls=%async_computation.2 | async-start | bytes 2621440 | tf_op jit(solution)/shard_map/reduce_scatter | solution.py:503
  9.3 1.3 copy-start.4
  9.4 1.6 copy-start.5
  201.1 1.3 copy-start.1
  202.4 2.2 copy-start.2
Sparse Core Ops, SparseCore 0:
  9.2 58.5 all-gather.1
  208.4 31.0 reduce-scatter.1

commit v4 on v3

--- a/solution.py
+++ b/solution.py
@@ -130,7 +130,7 @@
 
 def chain_kernel(
     last, x_ref, gain_ref, wq_ref, wk_ref, wv_ref, squares_ref, own_taps, out_ref,
-    xs, w_ref, acc, taps_ref, totals, prev, gates, shifted, stage, gath,
+    xs, w_rows, w_ref, acc, taps_ref, totals, prev, gates, shifted, stage, gath,
     w_sem, taps_send, taps_recv, sq_send, sq_recv,
     acc_send, acc_recv, x_send, x_recv, stage_send, stage_recv, z_send, z_recv,
 ):
@@ -151,7 +151,7 @@
     def w_copy(group, which):
         source = (wq_ref, wk_ref, wv_ref)[which]
         return pltpu.make_async_copy(
-            source.at[pl.ds(group * width, width)], w_ref.at[group, pl.ds(which * width, width)],
+            source.at[pl.ds(group * width, width)], w_rows.at[group, pl.ds(which * width, width)],
             w_sem.at[group, which],
         )
 
@@ -235,6 +235,10 @@
     for group in range(4):
         for which in range(3):
             w_copy(group, which).wait()
+
+    @pl.loop(0, 4)
+    def _(group):
+        w_ref[group] = jnp.transpose(w_rows[group])
 
     def wait_small():
         for source in range(2 * n_col):
@@ -291,9 +295,10 @@
         gates[part, 0:SUB, :] = gates[part, rows : rows + SUB, :]
         total = taps[9:10, :] * gate
         for move in range(SUB):
+            window = shifted[part, move]
             for back in range(0, FILTER_LEN, SUB):
                 row = 16 + back + move
-                total = total + taps[row : row + 1, :] * shifted[part, move, rows - back : 2 * rows - back, :]
+                total = total + taps[row : row + 1, :] * window[rows - back : 2 * rows - back, :]
         value = (filtered[0] * total).astype(jnp.bfloat16)
         spot = pl.ds(pl.multiple_of(place * rows, rows), rows)
 
@@ -336,7 +341,7 @@
                 part = lax.rem(chunk // pieces, 2)
                 own = lax.dot_general(
                     xs[chunk // (2 * pieces), lax.rem(chunk, pieces)], w_ref[2 * half + part],
-                    (((1,), (1,)), ((), ())), preferred_element_type=jnp.float32,
+                    (((1,), (0,)), ((), ())), preferred_element_type=jnp.float32,
                 )
 
                 @pl.when(hops == 0)
@@ -460,6 +465,7 @@
         scratch_shapes=[
             pltpu.VMEM((2, pieces, rows, features), jnp.bfloat16),
             pltpu.VMEM((4, 3 * width, features), jnp.bfloat16),
+            pltpu.VMEM((4, features, 3 * width), jnp.bfloat16),
             pltpu.VMEM((2, chunks, rows, 3 * width), jnp.bfloat16),
             pltpu.VMEM(taps.shape, jnp.float32),
             pltpu.VMEM((2 * (last + 1),) + squares.shape, jnp.float32),

time: 247 us -> 247 us (level)
  no operation moved by 1% of the time
where the time goes in v4:
time: 247 us; the launch traced here: 246 us
  Pallas kernels  190 us (77%)
  waiting for transfers between devices  31.4 us (13%)
  between operations  13.5 us (5%)
  local copies, waits for them, and re-layouts  7.21 us (3%)
  matrix products  3.68 us (1%)
    pallas_call x1, Pallas kernels, chain(): pl.pallas_call(functools.partial(chain_kernel, last), in_specs=[vmem, vme...  190 us
    reduce_scatter x1, waiting for transfers between devices, on_device_chain(): lax.psum_scatter(out_part.astype(jnp.bfloat16), 'row', scatter_dimension=...  31.4 us
    unnamed x22, local copies, waits for them, and re-layouts  5.1 us
  transfers between devices with their start and end apart: 2, of which 1 were waited for; matrix products, arithmetic and copies ran while one was open for 0% of the time, Pallas kernels for 77%

profile of v4, /device:TPU:0, one launch (start us, length us, event | category | flops | bytes accessed | tf_op | source)
XLA Modules:
  0.0 246.5 jit_solution(17240346350037377864)
XLA Ops:
  6.5 0.0 all-gather.2.cloned.1.call-start
  6.6 2.4 copy.16
  9.0 0.0 all-gather.2.cloned.1.call-update
  9.0 0.0 reduce-scatter.2.cloned.1.call-start
  9.1 0.0 copy-done.8
  9.1 0.0 copy-done.7
  9.1 0.1 copy.13
  9.2 0.1 copy.15
  9.3 0.0 copy-start.4
  9.4 0.0 copy-start.5
  9.4 0.1 pad.2.clone
  9.5 0.0 copy-done.9
  9.5 0.1 maximum_bitcast_fusion.own_taps
  9.6 0.5 multiply_reduce_fusion
  10.0 0.2 copy-done.3
  10.2 0.4 copy-done.4
  10.7 0.3 copy-done.5
  11.0 190.0 %shard_map.91 = bf16[1024,1024]{1,0:T(8,128)(2,1)S(1)} custom-call(bf16[1024,1024]{1,0:T(8,128)(2,1)S(1)} %copy-done, f32[1,1024]{1,0:T(1,128)S(1)} %bitcast.13, bf16[512,1024]{1,0:T(8,128)(2,1)S(1)} %copy-done.3, bf16[512,1024]{1,0:T(8,128)(2,1)S(1)} %copy-done.4, bf16[512,1024]{1,0:T(8,128)(2,1)S(1)} %copy-done.5, f32[8,128]{1,0:T(8,128)S(1)} %bitcast.12, ...), custom_call_target="tpu_custom_call" | custom-call | tf_op jit(solution)/shard_map/pallas_call | solution.py:460
  201.0 1.3 copy-done.1
  202.3 1.9 copy.17
  204.2 0.3 copy-done.2
  204.5 3.7 %convolution_convert_fusion = bf16[1024,1024]{1,0:T(8,128)(2,1)} fusion(bf16[1024,1024]{1,0:T(8,128)(2,1)S(1)} %copy-done.2, bf16[1024,1024]{0,1:T(8,128)(2,1)S(1)} %bitcast.15), kind=kOutput, calls=%fused_computation.1 | convolution fusion | flops 2148532224 | bytes 6291456 | tf_op jit(solution)/shard_map/dot_general | solution.py:506
  208.2 0.0 reduce-scatter.2.cloned.1.call-update
  208.2 31.4 %reduce-scatter.2.cloned.1.call-done = bf16[256,1024]{1,0:T(8,128)(2,1)} async-done(((bf16[1024,1024]{1,0:T(8,128)(2,1)}), bf16[256,1024]{1,0:T(8,128)(2,1)}) %reduce-scatter.2.cloned.1.call-update) | async-done | bytes 524304 | tf_op jit(solution)/shard_map/reduce_scatter | solution.py:509
  (14 shorter events, 0.0 us)
Async XLA Ops:
  6.5 2.6 %copy-start.8 = (f32[3,3,256]{2,1,0:T(4,128)S(1)}, f32[3,3,256]{2,1,0:T(4,128)}, u32[]{:S(2)}) copy-start(f32[3,3,256]{2,1,0:T(4,128)} %param.14) | copy-start | bytes 27652
  6.5 2.6 %copy-start.7 = (f32[128,256]{1,0:T(8,128)S(1)}, f32[128,256]{1,0:T(8,128)}, u32[]{:S(2)}) copy-start(f32[128,256]{1,0:T(8,128)} %param.15) | copy-start | bytes 393220
  6.5 2.9 %copy-start.9 = (f32[256]{0:T(256)S(1)}, f32[256]{0:T(256)}, u32[]{:S(2)}) copy-start(f32[256]{0:T(256)} %param.16) | copy-start | bytes 3076
  6.5 3.0 %copy-start = (bf16[1024,1024]{1,0:T(8,128)(2,1)S(1)}, bf16[1024,1024]{1,0:T(8,128)(2,1)}, u32[]{:S(2)}) copy-start(bf16[1024,1024]{1,0:T(8,128)(2,1)} %x_ref.1) | copy-start | bytes 6291460
  6.5 195.8 %all-gather.2.cloned.1.call-start = ((), (), s32[]{:S(2)}) async-start(), calls=%async_computation.1 | async-start | bytes 3145728 | tf_op jit(solution)/shard_map/all_gather | solution.py:499
  9.0 1.2 copy-start.3
  9.0 1.2 copy-start.6
  9.0 230.6 %reduce-scatter.2.cloned.1.call-start = ((), (), s32[]{:S(2)}) async-start(), calls=%async_computation.2 | async-start | bytes 2621440 | tf_op jit(solution)/shard_map/reduce_scatter | solution.py:509
  9.3 1.3 copy-start.4
  9.4 1.6 copy-start.5
  201.0 1.3 copy-start.1
  202.3 2.2 copy-start.2
Sparse Core Ops, SparseCore 0:
  9.2 58.4 all-gather.1
  208.4 31.2 reduce-scatter.1

commit v5 on v4

--- a/solution.py
+++ b/solution.py
@@ -126,6 +126,9 @@
 
 
 QUARTERS = 4
+SLACK = 2
+LATE = 2
+BLOCKS = 2
 
 
 def chain_kernel(
@@ -140,7 +143,7 @@
     rows = xs.shape[2]
     width = gath.shape[4]
     quarter = gath.shape[3] // QUARTERS
-    per = pieces // QUARTERS
+    group_len = pieces // BLOCKS
     n_col = last + 1
     is_end = (col == 0) | (col == last)
     end_half = jnp.where(col == 0, 0, 1)
@@ -210,10 +213,6 @@
         own_taps, taps_ref, taps_send, taps_recv, device_id={"col": taps_end}, device_id_type=mesh_ids
     )
 
-    @pl.loop(0, pieces)
-    def _(piece):
-        x_copy(piece).start()
-
     for far in range(2):
         for away in (0, last):
             @pl.when((col != away) if far == 0 else (col >= 0))
@@ -264,23 +263,23 @@
     )
 
     def filter_block(part, mine, place, again):
-        chunk = mine * 2 * pieces + part * pieces + place
+        chunk = mine * 2 * group_len + part * group_len + place // BLOCKS
+        held = pl.ds(pl.multiple_of(lax.rem(place, BLOCKS) * rows, rows), rows)
         half = lax.rem(ctx + mine, 2)
         row_scale = totals[half * n_col, pl.ds(place, 1), :]
         scale = jnp.sum(jnp.where(diagonal, row_scale, 0.0), axis=1, keepdims=True)
         taps = taps_ref.at[part]
 
-        if not again:
-            @pl.when((place == 0) & ((mine == 0) | (ctx == 1)))
-            def _():
-                prev[part] = jnp.zeros(prev.shape[1:], jnp.float32)
-                gates[part, 0:SUB, :] = jnp.zeros((SUB, width), jnp.float32)
-                shifted[part, :, rows:, :] = jnp.zeros((SUB, rows, width), jnp.float32)
+        @pl.when((place == 0) & ((mine == 0) | (ctx == 1)) & jnp.logical_not(again))
+        def _():
+            prev[part] = jnp.zeros(prev.shape[1:], jnp.float32)
+            gates[part, 0:SUB, :] = jnp.zeros((SUB, width), jnp.float32)
+            shifted[part, :, rows:, :] = jnp.zeros((SUB, rows, width), jnp.float32)
 
         shifted[part, :, 0:rows, :] = shifted[part, :, rows:, :]
         filtered = []
         for which in range(3):
-            now = acc[end_half, chunk, :, which * width : (which + 1) * width].astype(jnp.float32) * scale
+            now = acc[end_half, chunk, held, which * width : (which + 1) * width].astype(jnp.float32) * scale
             prev[part, which, SUB:, :] = now
             total = taps[3 * which : 3 * which + 1, :] * now
             for tap in range(1, SHORT_LEN):
@@ -324,40 +323,55 @@
         def _():
             z_copy(half, part, source, place).start()
 
-    @pl.loop(0, chunks + 4 * last)
+    @pl.loop(0, chunks + 2 * SLACK * last)
     def _(step):
-        first = step - 2 * jnp.minimum(col, last - col)
-
-        @pl.when((first >= 2 * pieces) & (first < 3 * pieces))
-        def _():
-            x_copy(first - 2 * pieces).wait_recv()
+        @pl.when(step < group_len)
+        def _():
+            for block in range(BLOCKS):
+                x_copy(step * BLOCKS + block).start()
+
+        first = step - SLACK * jnp.minimum(col, last - col)
+
+        @pl.when((first >= 2 * group_len) & (first < 3 * group_len))
+        def _():
+            for block in range(BLOCKS):
+                x_copy((first - 2 * group_len) * BLOCKS + block).wait_recv()
 
         for half in range(2):
             hops = last - col if half == 0 else col
-            chunk = step - 2 * hops
+            chunk = step - SLACK * hops
 
             @pl.when((chunk >= 0) & (chunk < chunks))
             def _():
-                part = lax.rem(chunk // pieces, 2)
-                own = lax.dot_general(
-                    xs[chunk // (2 * pieces), lax.rem(chunk, pieces)], w_ref[2 * half + part],
-                    (((1,), (0,)), ((), ())), preferred_element_type=jnp.float32,
-                )
-
-                @pl.when(hops == 0)
-                def _():
-                    acc[half, chunk] = own.astype(jnp.bfloat16)
+                part = lax.rem(chunk // group_len, 2)
 
                 @pl.when(hops > 0)
                 def _():
                     acc_copy(half, chunk).wait_recv()
-                    acc[half, chunk] = (own + acc[half, chunk].astype(jnp.float32)).astype(jnp.bfloat16)
+
+                @pl.loop(0, BLOCKS)
+                def _(block):
+                    place = lax.rem(chunk, group_len) * BLOCKS + block
+                    held = pl.ds(pl.multiple_of(block * rows, rows), rows)
+                    own = lax.dot_general(
+                        xs[chunk // (2 * group_len), place], w_ref[2 * half + part],
+                        (((1,), (0,)), ((), ())), preferred_element_type=jnp.float32,
+                    )
+
+                    @pl.when(hops == 0)
+                    def _():
+                        acc[half, chunk, held, :] = own.astype(jnp.bfloat16)
+
+                    @pl.when(hops > 0)
+                    def _():
+                        held_sum = acc[half, chunk, held, :].astype(jnp.float32)
+                        acc[half, chunk, held, :] = (own + held_sum).astype(jnp.bfloat16)
 
                 @pl.when(hops < last)
                 def _():
                     acc_copy(half, chunk).start()
 
-        done = step - 2 * last
+        done = step - SLACK * last
 
         @pl.when(is_end & (done == 0))
         def _():
@@ -365,37 +379,39 @@
 
         @pl.when(is_end & (done >= 0) & (done < chunks))
         def _():
-            mine, part, place = done // (2 * pieces), lax.rem(done // pieces, 2), lax.rem(done, pieces)
-            filter_block(part, mine, place, False)
-
-            @pl.when((mine == 1) & (lax.rem(place, per) == per - 1))
-            def _():
-                stage_copy(part, place // per).start()
-
-            @pl.when((mine == 1) & (place == pieces - 1) & (ctx == 1))
-            def _():
-                filter_block(part, 0, 0, True)
+            mine, part = done // (2 * group_len), lax.rem(done // group_len, 2)
+            place = lax.rem(done, group_len)
+            seam = (mine == 1) & (place == group_len - 1) & (ctx == 1)
+
+            @pl.loop(0, BLOCKS + jnp.where(seam, 1, 0))
+            def _(block):
+                again = block == BLOCKS
+                filter_block(
+                    part, jnp.where(again, 0, mine), jnp.where(again, 0, place * BLOCKS + block), again
+                )
+
+            @pl.when(mine == 1)
+            def _():
+                stage_copy(part, place).start()
 
         for half in range(2):
             hops = col if half == 0 else last - col
-            event = step - 2 * last - 2 * hops
-            full = lax.rem(event + per, per) == per - 1
-            index = event // per
-
-            @pl.when((event >= 0) & (event < 2 * pieces) & full)
-            def _():
-                place = lax.rem(index, QUARTERS)
+            event = step - SLACK * (last + hops)
+
+            @pl.when((event >= 0) & (event < 2 * group_len))
+            def _():
+                place = lax.rem(event, QUARTERS)
 
                 @pl.when((ctx == 0) | (place > 0))
                 def _():
-                    pass_on(half, hops, index // QUARTERS, ctx, place, False)
-
-            @pl.when((event >= 2 * pieces + per) & (event < chunks) & full)
-            def _():
-                late = index - 2 * QUARTERS - 1
+                    pass_on(half, hops, event // QUARTERS, ctx, place, False)
+
+            @pl.when((event >= 2 * group_len + LATE) & (event < chunks))
+            def _():
+                late = event - 2 * group_len - LATE
                 pass_on(half, hops, late // QUARTERS, 1 - ctx, lax.rem(late, QUARTERS), True)
 
-            @pl.when((event == 3 * pieces) & (ctx == 1))
+            @pl.when((event == 3 * group_len) & (ctx == 1))
             def _():
                 pass_on(half, hops, 0, ctx, 0, False)
 
@@ -405,7 +421,9 @@
         def _():
             pass_on(half, hops, 1, ctx, 0, False)
 
-        pass_on(half, hops, 1, 1 - ctx, QUARTERS - 1, True)
+    for place in range(QUARTERS - LATE, QUARTERS):
+        for half in range(2):
+            pass_on(half, col if half == 0 else last - col, 1, 1 - ctx, place, True)
 
     for half in range(2):
         for part in range(2):
@@ -452,7 +470,7 @@
     tokens, features = activations.shape
     rows = FILTER_LEN
     pieces = tokens // rows
-    chunks = 4 * pieces
+    chunks = 4 * pieces // BLOCKS
     width = weights[0].shape[0] // 4
     dma = pltpu.SemaphoreType.DMA
     vmem = pl.BlockSpec(memory_space=pltpu.VMEM)
@@ -466,7 +484,7 @@
             pltpu.VMEM((2, pieces, rows, features), jnp.bfloat16),
             pltpu.VMEM((4, 3 * width, features), jnp.bfloat16),
             pltpu.VMEM((4, features, 3 * width), jnp.bfloat16),
-            pltpu.VMEM((2, chunks, rows, 3 * width), jnp.bfloat16),
+            pltpu.VMEM((2, chunks, BLOCKS * rows, 3 * width), jnp.bfloat16),
             pltpu.VMEM(taps.shape, jnp.float32),
             pltpu.VMEM((2 * (last + 1),) + squares.shape, jnp.float32),
             pltpu.VMEM((2, 3, SUB + rows, width), jnp.float32),

time: 247 us -> 252 us (1.020)
  waiting for transfers between devices: 31.4 us -> 50.9 us
  Pallas kernels: 190 us -> 176 us
    reduce_scatter x1, waiting for transfers between devices: 31.4 us -> 50.9 us  [on_device_chain(): lax.psum_scatter(out_part.astype(jnp.bfloat16), 'row', scatter_dimension=...]
    pallas_call x1, Pallas kernels: 190 us -> 176 us  [chain(): pl.pallas_call(functools.partial(chain_kernel, last), in_specs=[vmem, vme...]
  transfers between devices with their start and end apart: 2 -> 2, of which waited for: 1 -> 1; matrix products, arithmetic and copies ran while one was open for 0% -> 0% of each run, Pallas kernels for 77% -> 70%
where the time goes in v5:
time: 252 us
  Pallas kernels  176 us (70%)
  waiting for transfers between devices  50.9 us (20%)
  between operations  13.5 us (5%)
  local copies, waits for them, and re-layouts  7.21 us (3%)
  matrix products  3.68 us (1%)
    pallas_call x1, Pallas kernels, chain(): pl.pallas_call(functools.partial(chain_kernel, last), in_specs=[vmem, vme...  176 us
    reduce_scatter x1, waiting for transfers between devices, on_device_chain(): lax.psum_scatter(out_part.astype(jnp.bfloat16), 'row', scatter_dimension=...  50.9 us
    unnamed x22, local copies, waits for them, and re-layouts  5.1 us
  transfers between devices with their start and end apart: 2, of which 1 were waited for; matrix products, arithmetic and copies ran while one was open for 0% of the time, Pallas kernels for 70%

profile of v5, /device:TPU:0, one launch (start us, length us, event | category | flops | bytes accessed | tf_op | source)
XLA Modules:
  0.0 251.6 jit_solution(9004262123246115879)
XLA Ops:
  6.5 0.0 all-gather.2.cloned.1.call-start
  6.6 2.4 copy.16
  9.0 0.0 all-gather.2.cloned.1.call-update
  9.0 0.0 reduce-scatter.2.cloned.1.call-start
  9.1 0.1 copy.13
  9.2 0.1 copy.15
  9.3 0.0 copy-start.4
  9.4 0.0 copy-start.5
  9.4 0.1 pad.2.clone
  9.5 0.0 copy-done.9
  9.5 0.1 maximum_bitcast_fusion.own_taps
  9.6 0.0 copy-done
  9.6 0.5 multiply_reduce_fusion
  10.0 0.2 copy-done.3
  10.2 0.0 copy-done.6
  10.2 0.4 copy-done.4
  10.7 0.3 copy-done.5
  11.0 175.6 %shard_map.91 = bf16[1024,1024]{1,0:T(8,128)(2,1)S(1)} custom-call(bf16[1024,1024]{1,0:T(8,128)(2,1)S(1)} %copy-done, f32[1,1024]{1,0:T(1,128)S(1)} %bitcast.13, bf16[512,1024]{1,0:T(8,128)(2,1)S(1)} %copy-done.3, bf16[512,1024]{1,0:T(8,128)(2,1)S(1)} %copy-done.4, bf16[512,1024]{1,0:T(8,128)(2,1)S(1)} %copy-done.5, f32[8,128]{1,0:T(8,128)S(1)} %bitcast.12, ...), custom_call_target="tpu_custom_call" | custom-call | tf_op jit(solution)/shard_map/pallas_call | solution.py:478
  186.6 1.3 copy-done.1
  187.9 1.9 copy.17
  189.8 0.3 copy-done.2
  190.1 3.7 %convolution_convert_fusion = bf16[1024,1024]{1,0:T(8,128)(2,1)} fusion(bf16[1024,1024]{1,0:T(8,128)(2,1)S(1)} %copy-done.2, bf16[1024,1024]{0,1:T(8,128)(2,1)S(1)} %bitcast.15), kind=kOutput, calls=%fused_computation.1 | convolution fusion | flops 2148532224 | bytes 6291456 | tf_op jit(solution)/shard_map/dot_general | solution.py:524
  193.8 0.0 reduce-scatter.2.cloned.1.call-update
  193.8 50.9 %reduce-scatter.2.cloned.1.call-done = bf16[256,1024]{1,0:T(8,128)(2,1)} async-done(((bf16[1024,1024]{1,0:T(8,128)(2,1)}), bf16[256,1024]{1,0:T(8,128)(2,1)}) %reduce-scatter.2.cloned.1.call-update) | async-done | bytes 524304 | tf_op jit(solution)/shard_map/reduce_scatter | solution.py:527
  (14 shorter events, 0.0 us)
Async XLA Ops:
  6.5 2.6 %copy-start.8 = (f32[3,3,256]{2,1,0:T(4,128)S(1)}, f32[3,3,256]{2,1,0:T(4,128)}, u32[]{:S(2)}) copy-start(f32[3,3,256]{2,1,0:T(4,128)} %param.14) | copy-start | bytes 27652
  6.5 2.6 %copy-start.7 = (f32[128,256]{1,0:T(8,128)S(1)}, f32[128,256]{1,0:T(8,128)}, u32[]{:S(2)}) copy-start(f32[128,256]{1,0:T(8,128)} %param.15) | copy-start | bytes 393220
  6.5 2.9 %copy-start.9 = (f32[256]{0:T(256)S(1)}, f32[256]{0:T(256)}, u32[]{:S(2)}) copy-start(f32[256]{0:T(256)} %param.16) | copy-start | bytes 3076
  6.5 3.0 %copy-start = (bf16[1024,1024]{1,0:T(8,128)(2,1)S(1)}, bf16[1024,1024]{1,0:T(8,128)(2,1)}, u32[]{:S(2)}) copy-start(bf16[1024,1024]{1,0:T(8,128)(2,1)} %x_ref.1) | copy-start | bytes 6291460
  6.5 181.4 %all-gather.2.cloned.1.call-start = ((), (), s32[]{:S(2)}) async-start(), calls=%async_computation.1 | async-start | bytes 3145728 | tf_op jit(solution)/shard_map/all_gather | solution.py:517
  9.0 1.2 copy-start.3
  9.0 1.2 copy-start.6
  9.0 235.7 %reduce-scatter.2.cloned.1.call-start = ((), (), s32[]{:S(2)}) async-start(), calls=%async_computation.2 | async-start | bytes 2621440 | tf_op jit(solution)/shard_map/reduce_scatter | solution.py:527
  9.3 1.3 copy-start.4
  9.4 1.6 copy-start.5
  186.6 1.3 copy-start.1
  187.9 2.2 copy-start.2
Sparse Core Ops, SparseCore 0:
  9.2 58.3 all-gather.1
  193.9 50.7 reduce-scatter.1
